TPU v7x, 32 devices: a whole 2x2x4 slice. The times are simulated.
32 devices in a mesh: grp: 2 (over y), seq: 8 (over z, core), dp: 2 (over x).
Axes of the slice: x: 2, y: 2, z: 4, core: 2. Of those that a mesh axis runs over, the one named last changes fastest.
Arguments:
- queries: bfloat16 [8, 2048, 2048], P(('grp', 'dp'), 'seq'), may hold values from -26 to 26
- key_states: bfloat16 [8, 2048, 2048], P(('grp', 'dp'), 'seq'), may hold values from -26 to 26
- value_states: bfloat16 [8, 2048, 2048], P(('grp', 'dp'), 'seq'), may hold values from -6 to 6
- projector: bfloat16 [2048, 1536], P('seq'), may hold values from -0.125 to 0.125
- teacher: bfloat16 [8, 2048, 1536], P(('grp', 'dp'), 'seq'), may hold values from -6 to 6
- enc_gain: float32 [1536], replicated, may hold values from 0.1 to 1.9
- enc_bias: float32 [1536], replicated, may hold values from -3 to 3
- valid_len: int32 [8], replicated, may hold values from 1 to 2048, 12288 in all
Outputs:
- grad_queries: bfloat16 [8, 2048, 2048], P(('grp', 'dp'), 'seq')
- grad_keys: bfloat16 [8, 2048, 2048], P(('grp', 'dp'), 'seq')
- grad_values: bfloat16 [8, 2048, 2048], P(('grp', 'dp'), 'seq')
Inputs may be any that keep to these rules, and one draw needn't show every extreme that they name: valid_len[b] counts the leading real tokens of image b; some image has all 2048.
All inputs are finite; a program needn't handle non-finite values.
Results may differ from a plain program's by a relative error of at most 0.025.
Values may be sent and summed in bfloat16 or wider, within the bound.
No kernel may reach another device: no remote copies, remote signals or barrier semaphores. Data moves between devices by JAX's collectives and lax.ppermute only.
A program may use at most 192 MiB of HBM per device.

v0:
```python
import jax
import jax.numpy as jnp
from jax import lax
from jax.sharding import PartitionSpec as P

HD = 128


EPS = 1e-06
COEF = 2048.0


def from_partner(value, axis, apart):
    return lax.ppermute(value, axis, [(i, i ^ 1 << apart) for i in range(lax.axis_size(axis))])


def layer_norm(rows, gain, bias):
    data = rows.astype(jnp.float32)
    center = data - jnp.mean(data, axis=-1, keepdims=True)
    spread = jnp.mean(center * center, axis=-1, keepdims=True)
    return center * lax.rsqrt(spread + EPS) * gain + bias


def cosine_grad(aligned, target, keep):
    tgt = target.astype(jnp.float32)
    width = aligned.shape[-1]
    inner = jnp.mean(aligned * tgt, axis=-1, keepdims=True)
    own = jnp.mean(aligned * aligned, axis=-1, keepdims=True) + EPS
    other = jnp.mean(tgt * tgt, axis=-1, keepdims=True) + EPS
    inverse = lax.rsqrt(own * other)
    cosine = inner * inverse
    return -COEF / width * keep[..., None] * (tgt * inverse - cosine / own * aligned)


def to_heads(rows, ranks):
    count, seg, width = rows.shape
    heads = width // HD
    split = rows.reshape(count, seg, heads, HD).transpose(0, 2, 1, 3)
    return split.reshape(ranks, count * heads // ranks, seg, HD)


def from_heads(block, count):
    ranks, per, seg, depth = block.shape
    heads = ranks * per // count
    return (
        block.reshape(count, heads, seg, depth)
        .transpose(0, 2, 1, 3)
        .reshape(count, seg, heads * depth)
    )


def attend(qh, kh, key_keep, scale):
    scores = jnp.einsum("pid,pjd->pij", qh, kh, preferred_element_type=jnp.float32) * scale
    scores = jnp.where(key_keep[:, None, :], scores, -jnp.inf)
    top = jnp.max(scores, axis=-1, keepdims=True)
    expo = jnp.exp(scores - top)
    return expo / jnp.sum(expo, axis=-1, keepdims=True)


def to_blocks(data, blocks):
    per, total, depth = data.shape
    return data.reshape(per, blocks, total // blocks, depth).transpose(1, 0, 2, 3)


def from_blocks(data):
    blocks, per, rows, depth = data.shape
    return data.transpose(1, 0, 2, 3).reshape(per, blocks * rows, depth)


def shards(queries, key_states, value_states, projector, teacher, enc_gain, enc_bias, valid_len):
    ranks = lax.axis_size("seq")
    count, seg, width = queries.shape
    heads = width // HD
    per = count * heads // ranks
    total = seg * ranks
    rows_block = min(512, total)
    blocks = total // rows_block
    scale = HD ** (-0.5)
    moved = from_partner(teacher, "grp", 0)
    target = layer_norm(moved, enc_gain, enc_bias).astype(jnp.bfloat16)
    first_image = (lax.axis_index("grp") * lax.axis_size("dp") + lax.axis_index("dp")) * count
    local_len = lax.dynamic_slice_in_dim(valid_len, first_image, count)
    token_pos = lax.axis_index("seq") * seg + jnp.arange(seg, dtype=jnp.int32)
    token_keep = (token_pos[None, :] < local_len[:, None]).astype(jnp.float32)
    pair_ids = lax.axis_index("seq") * per + jnp.arange(per, dtype=jnp.int32)
    pair_image = pair_ids // heads
    match = pair_image[:, None] == jnp.arange(count, dtype=jnp.int32)[None, :]
    pair_len = jnp.sum(jnp.where(match, local_len[None, :], 0), axis=1)
    key_keep = jnp.arange(total, dtype=jnp.int32)[None, :] < pair_len[:, None]
    q_in, k_in, v_in = (
        lax.all_to_all(to_heads(queries, ranks), "seq", split_axis=0, concat_axis=2, tiled=True),
        lax.all_to_all(to_heads(key_states, ranks), "seq", split_axis=0, concat_axis=2, tiled=True),
        lax.all_to_all(
            to_heads(value_states, ranks), "seq", split_axis=0, concat_axis=2, tiled=True
        ),
    )
    qh = q_in.reshape(per, total, HD)
    kh = k_in.reshape(per, total, HD)
    vh = v_in.reshape(per, total, HD)
    q_blocks = to_blocks(qh, blocks)

    def forward_block(q_part):
        probs = attend(q_part, kh, key_keep, scale)
        probs_b = probs.astype(jnp.bfloat16)
        attended = jnp.einsum(
            "pij,pjd->pid", probs_b, vh, preferred_element_type=jnp.float32
        ).astype(jnp.bfloat16)
        return (attended, probs)

    att_blocks, kept_probs = lax.map(forward_block, q_blocks)
    attended = from_blocks(att_blocks)
    back = lax.all_to_all(
        attended.reshape(1, per, total, HD), "seq", split_axis=2, concat_axis=0, tiled=True
    )
    att_rows = from_heads(back, count).reshape(count * seg, width)
    whole = lax.all_gather(projector, "seq", axis=0, tiled=True)
    aligned = jnp.dot(att_rows, whole, preferred_element_type=jnp.float32)
    grad_aligned = cosine_grad(
        aligned, target.reshape(count * seg, -1), token_keep.reshape(count * seg)
    ).astype(jnp.bfloat16)
    grad_att = jnp.dot(grad_aligned, whole.T, preferred_element_type=jnp.float32)
    grad_att = grad_att.astype(jnp.bfloat16).reshape(count, seg, width)
    g_in = lax.all_to_all(to_heads(grad_att, ranks), "seq", split_axis=0, concat_axis=2, tiled=True)
    gh = g_in.reshape(per, total, HD)
    g_blocks = to_blocks(gh, blocks)

    def backward_block(carry, probs, q_part, g_part):
        acc_k, acc_v = carry
        probs_b = probs.astype(jnp.bfloat16)
        acc_v = acc_v + jnp.einsum(
            "pij,pid->pjd", probs_b, g_part, preferred_element_type=jnp.float32
        )
        grad_probs = jnp.einsum("pid,pjd->pij", g_part, vh, preferred_element_type=jnp.float32)
        delta = jnp.sum(probs * grad_probs, axis=-1, keepdims=True)
        grad_scores = (probs * (grad_probs - delta) * scale).astype(jnp.bfloat16)
        grad_q = jnp.einsum(
            "pij,pjd->pid", grad_scores, kh, preferred_element_type=jnp.float32
        ).astype(jnp.bfloat16)
        acc_k = acc_k + jnp.einsum(
            "pij,pid->pjd", grad_scores, q_part, preferred_element_type=jnp.float32
        )
        return ((acc_k, acc_v), grad_q)

    start = (jnp.zeros((per, total, HD), jnp.float32), jnp.zeros((per, total, HD), jnp.float32))

    def step_kept(carry, items):
        probs, q_part, g_part = items
        return backward_block(carry, probs, q_part, g_part)

    (acc_k, acc_v), gq_blocks = lax.scan(step_kept, start, (kept_probs, q_blocks, g_blocks))
    grad_q = from_blocks(gq_blocks)
    grad_k = acc_k.astype(jnp.bfloat16)
    grad_v = acc_v.astype(jnp.bfloat16)
    gq_back, gk_back, gv_back = (
        lax.all_to_all(
            grad_q.reshape(1, per, total, HD), "seq", split_axis=2, concat_axis=0, tiled=True
        ),
        lax.all_to_all(
            grad_k.reshape(1, per, total, HD), "seq", split_axis=2, concat_axis=0, tiled=True
        ),
        lax.all_to_all(
            grad_v.reshape(1, per, total, HD), "seq", split_axis=2, concat_axis=0, tiled=True
        ),
    )
    return (from_heads(gq_back, count), from_heads(gk_back, count), from_heads(gv_back, count))


def solution(mesh):
    return jax.shard_map(
        shards,
        mesh=mesh,
        in_specs=(
            P(("grp", "dp"), "seq", None),
            P(("grp", "dp"), "seq", None),
            P(("grp", "dp"), "seq", None),
            P("seq", None),
            P(("grp", "dp"), "seq", None),
            P(),
            P(),
            P(),
        ),
        out_specs=(
            P(("grp", "dp"), "seq", None),
            P(("grp", "dp"), "seq", None),
            P(("grp", "dp"), "seq", None),
        ),
        check_vma=False,
    )
```

profile of v0, /device:TPU:13, one launch (start us, length us, event | category | flops | bytes accessed | tf_op | source)
XLA Modules:
  0.0 873.3 jit_solution(2248510583673375756)
XLA Ops:
  25.9 37.6 %all-to-all-done = bf16[8,4,256,128]{3,2,1,0:T(8,128)(2,1)S(1)} async-done(((bf16[8,4,256,128]{3,2,1,0:T(8,128)(2,1)}), bf16[8,4,256,128]{3,2,1,0:T(8,128)(2,1)S(1)}, u32[]{:S(2)}, u32[]{:S(2)}) %all-to-all-start) | async-done | bytes 2097184 | tf_op jit(solution)/shard_map/all_to_all | solution.py:91
  79.2 37.6 %all-to-all-done.1 = bf16[8,4,256,128]{3,2,1,0:T(8,128)(2,1)} async-done(((bf16[8,4,256,128]{3,2,1,0:T(8,128)(2,1)}), bf16[8,4,256,128]{3,2,1,0:T(8,128)(2,1)}, u32[]{:S(2)}, u32[]{:S(2)}) %all-to-all-start.1) | async-done | bytes 2097184 | tf_op jit(solution)/shard_map/all_to_all | solution.py:92
  130.4 82.0 %all-to-all-done.2 = bf16[8,4,256,128]{3,2,1,0:T(8,128)(2,1)} async-done(((bf16[8,4,256,128]{3,2,1,0:T(8,128)(2,1)}), bf16[8,4,256,128]{3,2,1,0:T(8,128)(2,1)}, u32[]{:S(2)}, u32[]{:S(2)}) %all-to-all-start.2) | async-done | bytes 2097184 | tf_op jit(solution)/shard_map/all_to_all | solution.py:93
  215.9 122.6 %while.28 = (s32[]{:T(128)}, bf16[4,4,512,128]{3,2,0,1:T(8,128)(2,1)}, f32[4,4,512,2048]{3,2,1,0:T(8,128)}, bf16[4,4,512,128]{3,2,1,0:T(8,128)(2,1)}, bf16[4,204...) while((s32[]{:T(128)}, ...), condition=%wide.region_4.5_spmd.clone, body=%wide.region_1.4_spmd.clone.sunk | while | flops 2177116160 | bytes 72394344 | solution.py:110
  216.0 9.8 %fusion.116 = (f32[4,512]{1,0:T(4,128)S(1)}, f32[4,512,2048]{2,1,0:T(8,128)}) fusion(pred[4,2048]{1,0:T(4,128)(4,1)S(1)} %iota_compare_fusion.2, bf16[4,2048,128]{2,1,0:T(8,128)(2,1)} %get-tuple-element.395, bf16[4,4,512,128]{3,2,1,0:T(8,128)(2,1)} %get-tuple-element.394, s32[]{:T(128)} %get-tuple-element.383), kind=kOutput, calls=%fused_computation.92.clone.1 | convolution fusion | flops 1090521088 | bytes 19415552 | tf_op jit(solution)/shard_map/while/body/eval_jaxpr/sub | solution.py:56
  234.7 11.8 %bitcast_dynamic-update-slice_fusion.2 = f32[4,4,512,2048]{3,2,1,0:T(8,128)} fusion(f32[4,4,512,2048]{3,2,1,0:T(8,128)} %get-tuple-element.385, s32[]{:T(128)} %get-tuple-element.383, f32[4,512,2048]{2,1,0:T(8,128)} %get-tuple-element.364, f32[4,512]{1,0:T(4,128)S(1)} %get-tuple-element.365), kind=kLoop, calls=%fused_computation.2.clone.1 | loop fusion | flops 4194304 | bytes 33563136 | tf_op jit(solution)/shard_map/while/body/jit(dynamic_update_index_in_dim)/dynamic_update_slice | solution.py:110
  246.7 9.8 %fusion.116 = (f32[4,512]{1,0:T(4,128)S(1)}, f32[4,512,2048]{2,1,0:T(8,128)}) fusion(pred[4,2048]{1,0:T(4,128)(4,1)S(1)} %iota_compare_fusion.2, bf16[4,2048,128]{2,1,0:T(8,128)(2,1)} %get-tuple-element.395, bf16[4,4,512,128]{3,2,1,0:T(8,128)(2,1)} %get-tuple-element.394, s32[]{:T(128)} %get-tuple-element.383), kind=kOutput, calls=%fused_computation.92.clone.1 | convolution fusion | flops 1090521088 | bytes 19415552 | tf_op jit(solution)/shard_map/while/body/eval_jaxpr/sub | solution.py:56
  265.4 11.8 %bitcast_dynamic-update-slice_fusion.2 = f32[4,4,512,2048]{3,2,1,0:T(8,128)} fusion(f32[4,4,512,2048]{3,2,1,0:T(8,128)} %get-tuple-element.385, s32[]{:T(128)} %get-tuple-element.383, f32[4,512,2048]{2,1,0:T(8,128)} %get-tuple-element.364, f32[4,512]{1,0:T(4,128)S(1)} %get-tuple-element.365), kind=kLoop, calls=%fused_computation.2.clone.1 | loop fusion | flops 4194304 | bytes 33563136 | tf_op jit(solution)/shard_map/while/body/jit(dynamic_update_index_in_dim)/dynamic_update_slice | solution.py:110
  277.3 9.8 %fusion.116 = (f32[4,512]{1,0:T(4,128)S(1)}, f32[4,512,2048]{2,1,0:T(8,128)}) fusion(pred[4,2048]{1,0:T(4,128)(4,1)S(1)} %iota_compare_fusion.2, bf16[4,2048,128]{2,1,0:T(8,128)(2,1)} %get-tuple-element.395, bf16[4,4,512,128]{3,2,1,0:T(8,128)(2,1)} %get-tuple-element.394, s32[]{:T(128)} %get-tuple-element.383), kind=kOutput, calls=%fused_computation.92.clone.1 | convolution fusion | flops 1090521088 | bytes 19415552 | tf_op jit(solution)/shard_map/while/body/eval_jaxpr/sub | solution.py:56
  296.0 11.8 %bitcast_dynamic-update-slice_fusion.2 = f32[4,4,512,2048]{3,2,1,0:T(8,128)} fusion(f32[4,4,512,2048]{3,2,1,0:T(8,128)} %get-tuple-element.385, s32[]{:T(128)} %get-tuple-element.383, f32[4,512,2048]{2,1,0:T(8,128)} %get-tuple-element.364, f32[4,512]{1,0:T(4,128)S(1)} %get-tuple-element.365), kind=kLoop, calls=%fused_computation.2.clone.1 | loop fusion | flops 4194304 | bytes 33563136 | tf_op jit(solution)/shard_map/while/body/jit(dynamic_update_index_in_dim)/dynamic_update_slice | solution.py:110
  307.9 9.8 %fusion.116 = (f32[4,512]{1,0:T(4,128)S(1)}, f32[4,512,2048]{2,1,0:T(8,128)}) fusion(pred[4,2048]{1,0:T(4,128)(4,1)S(1)} %iota_compare_fusion.2, bf16[4,2048,128]{2,1,0:T(8,128)(2,1)} %get-tuple-element.395, bf16[4,4,512,128]{3,2,1,0:T(8,128)(2,1)} %get-tuple-element.394, s32[]{:T(128)} %get-tuple-element.383), kind=kOutput, calls=%fused_computation.92.clone.1 | convolution fusion | flops 1090521088 | bytes 19415552 | tf_op jit(solution)/shard_map/while/body/eval_jaxpr/sub | solution.py:56
  326.6 11.8 %bitcast_dynamic-update-slice_fusion.2 = f32[4,4,512,2048]{3,2,1,0:T(8,128)} fusion(f32[4,4,512,2048]{3,2,1,0:T(8,128)} %get-tuple-element.385, s32[]{:T(128)} %get-tuple-element.383, f32[4,512,2048]{2,1,0:T(8,128)} %get-tuple-element.364, f32[4,512]{1,0:T(4,128)S(1)} %get-tuple-element.365), kind=kLoop, calls=%fused_computation.2.clone.1 | loop fusion | flops 4194304 | bytes 33563136 | tf_op jit(solution)/shard_map/while/body/jit(dynamic_update_index_in_dim)/dynamic_update_slice | solution.py:110
  351.0 35.6 %collective-permute-done = bf16[2,256,1536]{2,1,0:T(8,128)(2,1)} collective-permute-done((bf16[2,256,1536]{2,1,0:T(8,128)(2,1)}, bf16[2,256,1536]{2,1,0:T(8,128)(2,1)}, u32[]{:S(2)}, u32[]{:S(2)}) %collective-permute-start) | collective-permute-done | bytes 1572896 | tf_op jit(solution)/shard_map/ppermute | solution.py:14
  426.2 45.4 %all-to-all-done.4 = bf16[8,4,256,128]{3,2,1,0:T(8,128)(2,1)} async-done(((bf16[8,4,256,128]{3,2,1,0:T(8,128)(2,1)}), bf16[8,4,256,128]{3,2,1,0:T(8,128)(2,1)}, u32[]{:S(2)}, u32[]{:S(2)}) %all-to-all-start.4) | async-done | bytes 2097184 | tf_op jit(solution)/shard_map/all_to_all | solution.py:123
  476.5 208.2 %while.29 = (s32[]{:T(128)}, f32[4,2048,128]{2,1,0:T(8,128)}, f32[4,2048,128]{2,1,0:T(8,128)}, bf16[4,4,512,128]{3,2,0,1:T(8,128)(2,1)}, f32[4,4,512,2048]{3,2,1...) while((s32[]{:T(128)}, f32[4,2048,128]{2,1,0:T(8,128)}, ...), condition=%wide.region_12.13_spmd.clone, body=%wide.region_10.12_spmd.clone.sunk | while | flops 5394141184 | bytes 159912112 | solution.py:150
  476.5 10.9 %fusion.126 = f32[4,512,2048]{2,1,0:T(8,128)} fusion(f32[4,4,512,2048]{3,2,1,0:T(8,128)} %get-tuple-element.425, s32[]{:T(128)} %get-tuple-element.410, bf16[4,2048,128]{2,1,0:T(8,128)(2,1)S(1)} %get-tuple-element.427, bf16[4,4,512,128]{3,2,0,1:T(8,128)(2,1)} %get-tuple-element.426), kind=kOutput, calls=%fused_computation.26.clone.1 | convolution fusion | flops 1077940224 | bytes 36176896 | tf_op jit(solution)/shard_map/while/body/eval_jaxpr/sub | solution.py:135
  487.4 15.6 %fusion.127 = bf16[4,512,2048]{2,1,0:T(8,128)(2,1)} fusion(f32[4,512,2048]{2,1,0:T(8,128)} %fusion.126, f32[4,4,512,2048]{3,2,1,0:T(8,128)} %get-tuple-element.425, s32[]{:T(128)} %get-tuple-element.410, bf16[4,2048,128]{2,1,0:T(8,128)(2,1)S(1)} %get-tuple-element.427, bf16[4,4,512,128]{3,2,0,1:T(8,128)(2,1)} %get-tuple-element.426), kind=kOutput, calls=%fused_computation.31.clone.1 | convolution fusion | flops 1090519040 | bytes 44565504 | tf_op jit(solution)/shard_map/while/body/eval_jaxpr/pid,pjd->pij/dot_general | solution.py:133
  516.1 10.5 %select_add_fusion.5 = f32[4,2048,128]{2,1,0:T(8,128)} fusion(f32[4,2048,128]{2,1,0:T(8,128)} %get-tuple-element.412, f32[4,4,512,2048]{3,2,1,0:T(8,128)} %get-tuple-element.425, s32[]{:T(128)} %get-tuple-element.410, pred[]{:T(512)S(6)} %compare.10, bf16[4,4,512,128]{3,2,0,1:T(8,128)(2,1)} %get-tuple-element.426), kind=kOutput, calls=%fused_computation.34.clone.1 | convolution fusion | flops 1075838976 | bytes 17302528 | tf_op jit(solution)/shard_map/while/body/eval_jaxpr/pij,pid->pjd/dot_general | solution.py:130
  526.6 10.9 %fusion.126 = f32[4,512,2048]{2,1,0:T(8,128)} fusion(f32[4,4,512,2048]{3,2,1,0:T(8,128)} %get-tuple-element.425, s32[]{:T(128)} %get-tuple-element.410, bf16[4,2048,128]{2,1,0:T(8,128)(2,1)S(1)} %get-tuple-element.427, bf16[4,4,512,128]{3,2,0,1:T(8,128)(2,1)} %get-tuple-element.426), kind=kOutput, calls=%fused_computation.26.clone.1 | convolution fusion | flops 1077940224 | bytes 36176896 | tf_op jit(solution)/shard_map/while/body/eval_jaxpr/sub | solution.py:135
  537.5 15.6 %fusion.127 = bf16[4,512,2048]{2,1,0:T(8,128)(2,1)} fusion(f32[4,512,2048]{2,1,0:T(8,128)} %fusion.126, f32[4,4,512,2048]{3,2,1,0:T(8,128)} %get-tuple-element.425, s32[]{:T(128)} %get-tuple-element.410, bf16[4,2048,128]{2,1,0:T(8,128)(2,1)S(1)} %get-tuple-element.427, bf16[4,4,512,128]{3,2,0,1:T(8,128)(2,1)} %get-tuple-element.426), kind=kOutput, calls=%fused_computation.31.clone.1 | convolution fusion | flops 1090519040 | bytes 44565504 | tf_op jit(solution)/shard_map/while/body/eval_jaxpr/pid,pjd->pij/dot_general | solution.py:133
  567.5 11.8 %select_add_fusion.5 = f32[4,2048,128]{2,1,0:T(8,128)} fusion(f32[4,2048,128]{2,1,0:T(8,128)} %get-tuple-element.412, f32[4,4,512,2048]{3,2,1,0:T(8,128)} %get-tuple-element.425, s32[]{:T(128)} %get-tuple-element.410, pred[]{:T(512)S(6)} %compare.10, bf16[4,4,512,128]{3,2,0,1:T(8,128)(2,1)} %get-tuple-element.426), kind=kOutput, calls=%fused_computation.34.clone.1 | convolution fusion | flops 1075838976 | bytes 17302528 | tf_op jit(solution)/shard_map/while/body/eval_jaxpr/pij,pid->pjd/dot_general | solution.py:130
  579.3 10.9 %fusion.126 = f32[4,512,2048]{2,1,0:T(8,128)} fusion(f32[4,4,512,2048]{3,2,1,0:T(8,128)} %get-tuple-element.425, s32[]{:T(128)} %get-tuple-element.410, bf16[4,2048,128]{2,1,0:T(8,128)(2,1)S(1)} %get-tuple-element.427, bf16[4,4,512,128]{3,2,0,1:T(8,128)(2,1)} %get-tuple-element.426), kind=kOutput, calls=%fused_computation.26.clone.1 | convolution fusion | flops 1077940224 | bytes 36176896 | tf_op jit(solution)/shard_map/while/body/eval_jaxpr/sub | solution.py:135
  590.2 15.6 %fusion.127 = bf16[4,512,2048]{2,1,0:T(8,128)(2,1)} fusion(f32[4,512,2048]{2,1,0:T(8,128)} %fusion.126, f32[4,4,512,2048]{3,2,1,0:T(8,128)} %get-tuple-element.425, s32[]{:T(128)} %get-tuple-element.410, bf16[4,2048,128]{2,1,0:T(8,128)(2,1)S(1)} %get-tuple-element.427, bf16[4,4,512,128]{3,2,0,1:T(8,128)(2,1)} %get-tuple-element.426), kind=kOutput, calls=%fused_computation.31.clone.1 | convolution fusion | flops 1090519040 | bytes 44565504 | tf_op jit(solution)/shard_map/while/body/eval_jaxpr/pid,pjd->pij/dot_general | solution.py:133
  620.1 11.8 %select_add_fusion.5 = f32[4,2048,128]{2,1,0:T(8,128)} fusion(f32[4,2048,128]{2,1,0:T(8,128)} %get-tuple-element.412, f32[4,4,512,2048]{3,2,1,0:T(8,128)} %get-tuple-element.425, s32[]{:T(128)} %get-tuple-element.410, pred[]{:T(512)S(6)} %compare.10, bf16[4,4,512,128]{3,2,0,1:T(8,128)(2,1)} %get-tuple-element.426), kind=kOutput, calls=%fused_computation.34.clone.1 | convolution fusion | flops 1075838976 | bytes 17302528 | tf_op jit(solution)/shard_map/while/body/eval_jaxpr/pij,pid->pjd/dot_general | solution.py:130
  632.0 10.9 %fusion.126 = f32[4,512,2048]{2,1,0:T(8,128)} fusion(f32[4,4,512,2048]{3,2,1,0:T(8,128)} %get-tuple-element.425, s32[]{:T(128)} %get-tuple-element.410, bf16[4,2048,128]{2,1,0:T(8,128)(2,1)S(1)} %get-tuple-element.427, bf16[4,4,512,128]{3,2,0,1:T(8,128)(2,1)} %get-tuple-element.426), kind=kOutput, calls=%fused_computation.26.clone.1 | convolution fusion | flops 1077940224 | bytes 36176896 | tf_op jit(solution)/shard_map/while/body/eval_jaxpr/sub | solution.py:135
  642.9 15.6 %fusion.127 = bf16[4,512,2048]{2,1,0:T(8,128)(2,1)} fusion(f32[4,512,2048]{2,1,0:T(8,128)} %fusion.126, f32[4,4,512,2048]{3,2,1,0:T(8,128)} %get-tuple-element.425, s32[]{:T(128)} %get-tuple-element.410, bf16[4,2048,128]{2,1,0:T(8,128)(2,1)S(1)} %get-tuple-element.427, bf16[4,4,512,128]{3,2,0,1:T(8,128)(2,1)} %get-tuple-element.426), kind=kOutput, calls=%fused_computation.31.clone.1 | convolution fusion | flops 1090519040 | bytes 44565504 | tf_op jit(solution)/shard_map/while/body/eval_jaxpr/pid,pjd->pij/dot_general | solution.py:133
  672.8 11.8 %select_add_fusion.5 = f32[4,2048,128]{2,1,0:T(8,128)} fusion(f32[4,2048,128]{2,1,0:T(8,128)} %get-tuple-element.412, f32[4,4,512,2048]{3,2,1,0:T(8,128)} %get-tuple-element.425, s32[]{:T(128)} %get-tuple-element.410, pred[]{:T(512)S(6)} %compare.10, bf16[4,4,512,128]{3,2,0,1:T(8,128)(2,1)} %get-tuple-element.426), kind=kOutput, calls=%fused_computation.34.clone.1 | convolution fusion | flops 1075838976 | bytes 17302528 | tf_op jit(solution)/shard_map/while/body/eval_jaxpr/pij,pid->pjd/dot_general | solution.py:130
  687.1 10.9 %copy.184 = bf16[4,2048,128]{2,0,1:T(4,128)(2,1)} copy(bf16[4,2048,128]{2,1,0:T(8,128)(2,1)S(1)} %convert_element_type.60) | data formatting | bytes 4194304
  707.7 10.8 %copy.183 = bf16[4,2048,128]{2,0,1:T(4,128)(2,1)} copy(bf16[4,2048,128]{2,1,0:T(8,128)(2,1)S(1)} %convert_element_type.61) | data formatting | bytes 4194304
  718.5 32.3 %all-to-all-done.6 = bf16[1,4,2048,128]{3,1,0,2:T(4,128)(2,1)S(1)} async-done(((bf16[1,4,2048,128]{3,1,0,2:T(4,128)(2,1)}), bf16[1,4,2048,128]{3,1,0,2:T(4,128)(2,1)S(1)}, u32[]{:S(2)}, u32[]{:S(2)}) %all-to-all-start.6) | async-done | bytes 2097184 | tf_op jit(solution)/shard_map/all_to_all | solution.py:158
  763.5 40.8 %all-to-all-done.7 = bf16[1,4,2048,128]{3,1,0,2:T(4,128)(2,1)} async-done(((bf16[1,4,2048,128]{3,1,0,2:T(4,128)(2,1)}), bf16[1,4,2048,128]{3,1,0,2:T(4,128)(2,1)}, u32[]{:S(2)}, u32[]{:S(2)}) %all-to-all-start.7) | async-done | bytes 2097184 | tf_op jit(solution)/shard_map/all_to_all | solution.py:161
  827.7 30.0 %all-to-all-done.5 = bf16[1,4,2048,128]{3,1,0,2:T(4,128)(2,1)} async-done(((bf16[1,4,2048,128]{3,1,0,2:T(4,128)(2,1)}), bf16[1,4,2048,128]{3,1,0,2:T(4,128)(2,1)}, u32[]{:S(2)}, u32[]{:S(2)}) %all-to-all-start.5) | async-done | bytes 2097184 | tf_op jit(solution)/shard_map/all_to_all | solution.py:155
  (103 shorter events, 257.3 us)
Async XLA Ops:
  12.4 51.1 %all-to-all-start = ((bf16[8,4,256,128]{3,2,1,0:T(8,128)(2,1)}), bf16[8,4,256,128]{3,2,1,0:T(8,128)(2,1)S(1)}, u32[]{:S(2)}, u32[]{:S(2)}) async-start(bf16[8,4,256,128]{3,2,1,0:T(8,128)(2,1)} %bitcast.213), calls=%async_computation | async-start | bytes 4194304 | tf_op jit(solution)/shard_map/all_to_all | solution.py:91
  63.6 53.3 %all-to-all-start.1 = ((bf16[8,4,256,128]{3,2,1,0:T(8,128)(2,1)}), bf16[8,4,256,128]{3,2,1,0:T(8,128)(2,1)}, u32[]{:S(2)}, u32[]{:S(2)}) async-start(bf16[8,4,256,128]{3,2,1,0:T(8,128)(2,1)} %bitcast.209), calls=%async_computation.1 | async-start | bytes 4194304 | tf_op jit(solution)/shard_map/all_to_all | solution.py:92
  79.2 46.3 %copy-start.6 = (s32[8]{0:T(128)S(1)}, s32[8]{0:T(128)}, u32[]{:S(2)}) copy-start(s32[8]{0:T(128)} %param.19) | copy-start | bytes 100
  116.8 95.6 %all-to-all-start.2 = ((bf16[8,4,256,128]{3,2,1,0:T(8,128)(2,1)}), bf16[8,4,256,128]{3,2,1,0:T(8,128)(2,1)}, u32[]{:S(2)}, u32[]{:S(2)}) async-start(bf16[8,4,256,128]{3,2,1,0:T(8,128)(2,1)} %bitcast.208), calls=%async_computation.2 | async-start | bytes 4194304 | tf_op jit(solution)/shard_map/all_to_all | solution.py:93
  124.7 276.1 %all-gather.2.cloned.1.call-start = ((), (), s32[]{:S(2)}) async-start(), calls=%async_computation.8 | async-start | bytes 7077888 | tf_op jit(solution)/shard_map/all_gather | solution.py:116
  125.6 1.7 copy-start.4
  343.1 7.9 copy-start.5
  343.1 47.2 %copy-start.2 = (f32[1536]{0:T(1024)S(1)}, f32[1536]{0:T(1024)}, u32[]{:S(2)}) copy-start(f32[1536]{0:T(1024)} %param.18) | copy-start | bytes 18436
  343.1 47.2 %copy-start.3 = (f32[1536]{0:T(1024)S(1)}, f32[1536]{0:T(1024)}, u32[]{:S(2)}) copy-start(f32[1536]{0:T(1024)} %param.17) | copy-start | bytes 18436
  343.1 53.0 %all-to-all-start.3 = ((bf16[1,4,2048,128]{3,1,0,2:T(4,128)(2,1)}), bf16[1,4,2048,128]{3,1,0,2:T(4,128)(2,1)}, u32[]{:S(2)}, u32[]{:S(2)}) async-start(bf16[1,4,2048,128]{3,1,0,2:T(4,128)(2,1)} %copy.138), calls=%async_computation.3 | async-start | bytes 4194304 | tf_op jit(solution)/shard_map/all_to_all | solution.py:112
  350.6 36.0 %collective-permute-start = (bf16[2,256,1536]{2,1,0:T(8,128)(2,1)}, bf16[2,256,1536]{2,1,0:T(8,128)(2,1)}, u32[]{:S(2)}, u32[]{:S(2)}) collective-permute-start(bf16[2,256,1536]{2,1,0:T(8,128)(2,1)} %param.16), channel_id=1, source_target_pairs={{0,16},{16,0},{1,17},{17,1},{2,18},{18,2},{3,19},{19,3},{4,20},{20... | collective-permute-start | bytes 4718600 | tf_op jit(solution)/shard_map/ppermute | solution.py:14
  408.4 3.3 copy-start.1
  417.8 53.8 %all-to-all-start.4 = ((bf16[8,4,256,128]{3,2,1,0:T(8,128)(2,1)}), bf16[8,4,256,128]{3,2,1,0:T(8,128)(2,1)}, u32[]{:S(2)}, u32[]{:S(2)}) async-start(bf16[8,4,256,128]{3,2,1,0:T(8,128)(2,1)} %bitcast.214), calls=%async_computation.4 | async-start | bytes 4194304 | tf_op jit(solution)/shard_map/all_to_all | solution.py:123
  503.0 8.3 copy-start
  553.1 9.6 %copy-start = (bf16[4,512,2048]{2,1,0:T(8,128)(2,1)S(1)}, bf16[4,512,2048]{2,1,0:T(8,128)(2,1)}, u32[]{:S(2)}) copy-start(bf16[4,512,2048]{2,1,0:T(8,128)(2,1)} %fusion.127) | copy-start | bytes 25165828 | tf_op jit(solution)/shard_map/while
  605.8 9.6 %copy-start = (bf16[4,512,2048]{2,1,0:T(8,128)(2,1)S(1)}, bf16[4,512,2048]{2,1,0:T(8,128)(2,1)}, u32[]{:S(2)}) copy-start(bf16[4,512,2048]{2,1,0:T(8,128)(2,1)} %fusion.127) | copy-start | bytes 25165828 | tf_op jit(solution)/shard_map/while
  658.5 9.6 %copy-start = (bf16[4,512,2048]{2,1,0:T(8,128)(2,1)S(1)}, bf16[4,512,2048]{2,1,0:T(8,128)(2,1)}, u32[]{:S(2)}) copy-start(bf16[4,512,2048]{2,1,0:T(8,128)(2,1)} %fusion.127) | copy-start | bytes 25165828 | tf_op jit(solution)/shard_map/while
  698.0 52.7 %all-to-all-start.6 = ((bf16[1,4,2048,128]{3,1,0,2:T(4,128)(2,1)}), bf16[1,4,2048,128]{3,1,0,2:T(4,128)(2,1)S(1)}, u32[]{:S(2)}, u32[]{:S(2)}) async-start(bf16[1,4,2048,128]{3,1,0,2:T(4,128)(2,1)} %bitcast.212), calls=%async_computation.6 | async-start | bytes 4194304 | tf_op jit(solution)/shard_map/all_to_all | solution.py:158
  750.7 53.5 %all-to-all-start.7 = ((bf16[1,4,2048,128]{3,1,0,2:T(4,128)(2,1)}), bf16[1,4,2048,128]{3,1,0,2:T(4,128)(2,1)}, u32[]{:S(2)}, u32[]{:S(2)}) async-start(bf16[1,4,2048,128]{3,1,0,2:T(4,128)(2,1)} %bitcast.210), calls=%async_computation.7 | async-start | bytes 4194304 | tf_op jit(solution)/shard_map/all_to_all | solution.py:161
  804.3 53.4 %all-to-all-start.5 = ((bf16[1,4,2048,128]{3,1,0,2:T(4,128)(2,1)}), bf16[1,4,2048,128]{3,1,0,2:T(4,128)(2,1)}, u32[]{:S(2)}, u32[]{:S(2)}) async-start(bf16[1,4,2048,128]{3,1,0,2:T(4,128)(2,1)} %copy.147), calls=%async_computation.5 | async-start | bytes 4194304 | tf_op jit(solution)/shard_map/all_to_all | solution.py:155
Sparse Core Ops, SparseCore 0:
  127.2 95.0 all-gather.1
where the time goes:
time: 887 us; the launch traced here: 873 us
  waiting for transfers between devices  346 us (39%)
  matrix products  294 us (33%)
  local copies, waits for them, and re-layouts  97 us (11%)
  other arithmetic  61.3 us (7%)
  starting transfers between devices  60.7 us (7%)
  between operations  14.5 us (2%)
    all_to_all x1, waiting for transfers between devices, shards(): lax.all_to_all(to_heads(value_states, ranks), 'seq', split_axis=0, concat...  82 us
    dot_general x4, matrix products, backward_block(): jnp.einsum('pid,pjd->pij', g_part, vh, preferred_element_type=jnp.float32)  62.4 us
    dynamic_update_slice x4, other arithmetic, shards(): att_blocks, kept_probs = lax.map(forward_block, q_blocks)  47.3 us
    unnamed x24, local copies, waits for them, and re-layouts  47 us
    dot_general x4, matrix products, backward_block(): jnp.einsum('pij,pid->pjd', probs_b, g_part, preferred_element_type=jnp.fl...  46 us
    all_to_all x1, waiting for transfers between devices, shards(): lax.all_to_all(to_heads(grad_att, ranks), 'seq', split_axis=0, concat_axi...  45.4 us
    sub x4, matrix products, backward_block(): grad_scores = (probs * (grad_probs - delta) * scale).astype(jnp.bfloat16)  43.6 us
    all_to_all x1, waiting for transfers between devices, shards(): lax.all_to_all(grad_v.reshape(1, per, total, HD), 'seq', split_axis=2, co...  40.8 us
  transfers between devices with their start and end apart: 10, of which 9 were waited for; matrix products, arithmetic and copies ran while one was open for 22% of the time, Pallas kernels for 0%

commit v1 on v0

v1 whole, which is shorter than its diff:
```python
import functools

import jax
import jax.numpy as jnp
from jax import lax
from jax.experimental import pallas as pl
from jax.experimental.pallas import tpu as pltpu
from jax.sharding import PartitionSpec as P

HD = 128
EPS = 1e-06
COEF = 2048.0
SCALE = HD ** (-0.5)
LOG2E = 1.4426950408889634
NEG = -1e30
NT = (((1,), (1,)), ((), ()))
NN = (((1,), (0,)), ((), ()))
VMEM_LIMIT = 62 * 1024 * 1024
VMEM_LIMIT_PLACE = 16 * 1024 * 1024
WEIGHT = 16


def dot(a, b, dims):
    return lax.dot_general(a, b, dims, preferred_element_type=jnp.float32)


def cost(flops, data, exps=0):
    return pl.CostEstimate(
        flops=WEIGHT * flops, bytes_accessed=WEIGHT * data, transcendentals=WEIGHT * exps
    )


def from_partner(value, axis, apart):
    return lax.ppermute(value, axis, [(i, i ^ 1 << apart) for i in range(lax.axis_size(axis))])


def exchange(slabs):
    if len(slabs) == 1:
        return [lax.all_to_all(slabs[0], "seq", split_axis=0, concat_axis=0, tiled=True)]
    ranks = len(slabs)
    return [
        lax.ppermute(slab, "seq", [(i, i ^ s) for i in range(ranks)]) if s else slab
        for s, slab in enumerate(slabs)
    ]


def slab_shapes(split, ranks, shape, dtype=jnp.bfloat16):
    if split:
        return [jax.ShapeDtypeStruct(shape, dtype)] * ranks
    return [jax.ShapeDtypeStruct((ranks,) + shape, dtype)]


def slab_specs(split, ranks, shape, index):
    if split:
        return [pl.BlockSpec(shape, index)] * ranks
    return [pl.BlockSpec((ranks,) + shape, lambda *at: (0,) + index(*at))]


def each_slab(refs, ranks, me):
    if len(refs) == 1:
        return [(s, refs[0].at[s]) for s in range(ranks)]
    return [(s ^ me, refs[s]) for s in range(ranks)]


def unread(deps):
    return [pl.BlockSpec(memory_space=pl.ANY)] * len(deps)


def image_at(plan, len_ref, me_ref):
    c, chunks, images = plan
    if chunks != 2 or images != 1:
        return c * images
    swap = (len_ref[me_ref[2] + 1] < len_ref[me_ref[2]]).astype(jnp.int32)
    return 1 - swap if c else swap


def span(rank, size):
    if isinstance(rank, int):
        return pl.ds(rank * size, size)
    return pl.ds(pl.multiple_of(rank * size, size), size)


def pack_kernel(per, parts, _, __, *refs):
    ins, out = refs[:parts], refs[-1]
    for part in range(parts):
        for r in range(out.shape[0]):
            for j in range(per):
                at = (r * per + j) * HD
                out[r, part, j] = ins[part][0, :, at : at + HD]


def pack_slabs_kernel(per, parts, ranks, _, __, *refs):
    ins, outs = refs[: ranks * parts], refs[-ranks:]
    for s in range(ranks):
        for part in range(parts):
            for j in range(per):
                outs[s][part, j] = ins[s * parts + part][0, :, j * HD : (j + 1) * HD]


def pack(arrays, plan, ranks, per, split, where, deps):
    seg, width = arrays[0].shape[1:]
    parts, images = len(arrays), plan[2]
    ranks_image = ranks // images
    if split:
        steps = 2 if seg % 32 == 0 else 1
        rows = seg // steps

        def column(s):
            return pl.BlockSpec(
                (1, rows, per * HD),
                lambda h, n, m: (
                    image_at(plan, n, m) + lax.div(m[0] ^ s, ranks_image),
                    h,
                    lax.rem(m[0] ^ s, ranks_image),
                ),
            )

        kernel = functools.partial(pack_slabs_kernel, per, parts, ranks)
        operands = list(arrays) * ranks
        in_specs = [column(s) for s in range(ranks) for _ in range(parts)]
        out_specs = slab_specs(split, ranks, (parts, per, rows, HD), lambda h, n, m: (0, 0, h, 0))
    else:
        group = 2 if ranks_image % 2 == 0 else 1
        steps_image = ranks_image // group
        steps = ranks // group
        kernel = functools.partial(pack_kernel, per, parts)
        operands = list(arrays)
        in_specs = [
            pl.BlockSpec(
                (1, seg, group * per * HD),
                lambda s, n, m: (
                    image_at(plan, n, m) + lax.div(s, steps_image),
                    0,
                    lax.rem(s, steps_image),
                ),
            )
        ] * parts
        out_specs = [
            pl.BlockSpec((group, parts, per, seg, HD), lambda s, n, m: (s, 0, 0, 0, 0))
        ]
    return pl.pallas_call(
        kernel,
        grid_spec=pltpu.PrefetchScalarGridSpec(
            num_scalar_prefetch=2,
            grid=(steps,),
            in_specs=in_specs + unread(deps),
            out_specs=out_specs,
        ),
        out_shape=slab_shapes(split, ranks, (parts, per, seg, HD)),
        cost_estimate=cost(0, 4 * parts * images * seg * width),
        compiler_params=pltpu.CompilerParams(vmem_limit_bytes=VMEM_LIMIT),
        name="pack",
    )(*where, *operands, *deps)


def unpack_kernel(per, parts, _, __, *refs):
    src, outs = refs[0], refs[-parts:]
    for part in range(parts):
        for r in range(src.shape[0]):
            for j in range(per):
                at = (r * per + j) * HD
                outs[part][0, :, at : at + HD] = src[r, part, j]


def unpack(block, plan, count, where, held, deps):
    ranks, parts, per, seg, _ = block.shape
    images = plan[2]
    width = ranks * per // images * HD
    ranks_image = ranks // images
    group = 2 if ranks_image % 2 == 0 else 1
    steps_image = ranks_image // group
    held = list(held)

    def at(s, n, m):
        image = image_at(plan, n, m) + lax.div(s, steps_image)
        return image, 0, lax.rem(s, steps_image)

    return pl.pallas_call(
        functools.partial(unpack_kernel, per, parts),
        grid_spec=pltpu.PrefetchScalarGridSpec(
            num_scalar_prefetch=2,
            grid=(ranks // group,),
            in_specs=[
                pl.BlockSpec((group, parts, per, seg, HD), lambda s, n, m: (s, 0, 0, 0, 0))
            ]
            + unread(held)
            + unread(deps),
            out_specs=[pl.BlockSpec((1, seg, group * per * HD), at)] * parts,
        ),
        out_shape=[jax.ShapeDtypeStruct((count, seg, width), jnp.bfloat16)] * parts,
        input_output_aliases={3 + i: i for i in range(len(held))},
        cost_estimate=cost(0, 4 * parts * images * seg * width),
        compiler_params=pltpu.CompilerParams(vmem_limit_bytes=VMEM_LIMIT),
        name="unpack",
    )(*where, block, *held, *deps)


def place_kernel(per, parts, _, __, src, *refs):
    for part in range(parts):
        for j in range(per):
            refs[parts + part][0, :, j * HD : (j + 1) * HD] = src[part, j]


def place(slab, distance, plan, count, ranks, where, held):
    parts, per, seg, _ = slab.shape
    images = plan[2]
    width = ranks * per // images * HD
    ranks_image = ranks // images

    def at(s, n, m):
        owner = m[0] ^ distance
        image = image_at(plan, n, m) + lax.div(owner, ranks_image)
        return image, 0, lax.rem(owner, ranks_image)

    return pl.pallas_call(
        functools.partial(place_kernel, per, parts),
        grid_spec=pltpu.PrefetchScalarGridSpec(
            num_scalar_prefetch=2,
            grid=(1,),
            in_specs=[pl.BlockSpec((parts, per, seg, HD), lambda s, n, m: (0, 0, 0, 0))]
            + unread(held),
            out_specs=[pl.BlockSpec((1, seg, per * HD), at)] * parts,
        ),
        out_shape=[jax.ShapeDtypeStruct((count, seg, width), jnp.bfloat16)] * parts,
        input_output_aliases={3 + i: i for i in range(parts)},
        cost_estimate=cost(0, 4 * parts * per * seg * HD),
        compiler_params=pltpu.CompilerParams(vmem_limit_bytes=VMEM_LIMIT_PLACE),
        name="place",
    )(*where, slab, *held)


def tiles_of(total, seg):
    return min(total, max(512, seg)), min(total, max(512, seg))


def for_each_count(count, most, body):
    for n in range(1, most + 1):
        pl.when(count == n)(functools.partial(body, n))


def pair_length(len_ref, me_ref, plan, heads):
    pair = me_ref[0] * pl.num_programs(0) + pl.program_id(0)
    return len_ref[me_ref[2] + image_at(plan, len_ref, me_ref) + lax.div(pair, heads)]


def forward_kernel(sizes, len_ref, me_ref, *refs):
    n_slabs, n_deps, ranks, seg, tq, tk, plan, heads = sizes
    ins, refs = refs[:n_slabs], refs[n_slabs + n_deps :]
    outs = refs[:n_slabs]
    st_ref, ot_ref, q_ref, k_ref, v_ref, vt_ref, even_ref, odd_ref, o_ref = refs[n_slabs:]
    length = pair_length(len_ref, me_ref, plan, heads)
    total = ranks * seg
    for r, slab in each_slab(ins, ranks, me_ref[0]):
        rows = span(r, seg)
        q_ref[rows, :] = slab[0]
        k_ref[rows, :] = slab[1]
        v_ref[rows, :] = slab[2]
    for t in range(total // tk):
        vt_ref[:HD, t * tk : (t + 1) * tk] = v_ref[t * tk : (t + 1) * tk, :].T
    vt_ref[HD:, :] = jnp.ones_like(vt_ref[HD:, :])
    nq = lax.div(length + (tq - 1), tq)
    nk = lax.div(length + (tk - 1), tk)

    last_step = total // tq - 1

    def with_tiles(tiles):
        def scores(i, s_ref, t, top):
            rows = slice(t * tk, (t + 1) * tk)
            s = dot(k_ref[rows, :], q_ref[span(i, tq), :], NT)
            if t == tiles - 1:
                row = lax.broadcasted_iota(jnp.int32, (tk, tq), 0) + t * tk
                s = jnp.where(row < length, s, NEG)
            s_ref[rows, :] = s
            high = jnp.max(s, axis=0, keepdims=True)
            return high if top is None else jnp.maximum(top, high)

        def q_step(i, top, s_ref, next_ref):
            acc, next_top = jnp.zeros((vt_ref.shape[0], tq), jnp.float32), None
            for t in range(tiles):
                rows = slice(t * tk, (t + 1) * tk)
                next_top = scores(jnp.minimum(i + 1, last_step), next_ref, t, next_top)
                p = jnp.exp2((s_ref[rows, :] - top) * (SCALE * LOG2E))
                acc = acc + dot(vt_ref[:, rows], p.astype(jnp.bfloat16), NN)
            denom = acc[HD : HD + 1]
            out = acc[:HD] * (1.0 / denom)
            st_ref[0:1, span(i, tq)] = top * (SCALE * LOG2E) + jnp.log2(denom)
            ot_ref[:, span(i, tq)] = out
            o_ref[span(i, tq), :] = out.T.astype(jnp.bfloat16)
            return next_top

        def two_steps(pair, top):
            top = q_step(2 * pair, top, even_ref, odd_ref)
            if last_step == 0:
                return top
            return q_step(2 * pair + 1, top, odd_ref, even_ref)

        top = None
        for t in range(tiles):
            top = scores(0, even_ref, t, top)
        lax.fori_loop(0, lax.div(nq + 1, 2), two_steps, top)

    for_each_count(nk, total // tk, with_tiles)

    def blank(i, _):
        o_ref[span(i, tq), :] = jnp.zeros((tq, HD), jnp.bfloat16)
        return 0

    lax.fori_loop(nq, total // tq, blank, 0)
    for r, slab in each_slab(outs, ranks, me_ref[0]):
        slab[...] = o_ref[span(r, seg), :]


def forward(qkv, plan, ranks, where, deps):
    split = len(qkv) > 1
    per, seg = qkv[0].shape[-3:-1]
    heads = ranks * per // plan[2]
    total = ranks * seg
    tq, tk = tiles_of(total, seg)
    *attended, stats, kept = pl.pallas_call(
        functools.partial(forward_kernel, (len(qkv), len(deps), ranks, seg, tq, tk, plan, heads)),
        grid_spec=pltpu.PrefetchScalarGridSpec(
            num_scalar_prefetch=2,
            grid=(per,),
            in_specs=slab_specs(split, ranks, (3, None, seg, HD), lambda p, n, m: (0, p, 0, 0))
            + unread(deps),
            out_specs=slab_specs(split, ranks, (None, seg, HD), lambda p, n, m: (p, 0, 0))
            + [
                pl.BlockSpec((None, 8, total), lambda p, n, m: (p, 0, 0)),
                pl.BlockSpec((None, HD, total), lambda p, n, m: (p, 0, 0)),
            ],
            scratch_shapes=[pltpu.VMEM((total, HD), jnp.bfloat16)] * 3
            + [
                pltpu.VMEM((HD + 16, total), jnp.bfloat16),
                pltpu.VMEM((total, tq), jnp.float32),
                pltpu.VMEM((total, tq), jnp.float32),
                pltpu.VMEM((total, HD), jnp.bfloat16),
            ],
        ),
        out_shape=slab_shapes(split, ranks, (per, seg, HD))
        + [
            jax.ShapeDtypeStruct((per, 8, total), jnp.float32),
            jax.ShapeDtypeStruct((per, HD, total), jnp.float32),
        ],
        cost_estimate=cost(8 * per * total * total * HD, 8 * per * total * HD, per * total * total),
        compiler_params=pltpu.CompilerParams(vmem_limit_bytes=VMEM_LIMIT),
        name="attend_fwd",
    )(*where, *qkv, *deps)
    return attended, (stats, kept)


def backward_kernel(sizes, len_ref, me_ref, *refs):
    n_slabs, n_deps, ranks, seg, tq, tk, plan, heads = sizes
    ins, g_ins = refs[:n_slabs], refs[n_slabs : 2 * n_slabs]
    st_ref, ot_ref = refs[2 * n_slabs : 2 * n_slabs + 2]
    refs = refs[2 * n_slabs + 2 + n_deps :]
    outs = refs[:n_slabs]
    q_ref, k_ref, v_ref, g_ref, kt_ref, dq_ref, dk_ref, dv_ref = refs[n_slabs:]
    length = pair_length(len_ref, me_ref, plan, heads)
    total = ranks * seg
    for r, slab in each_slab(ins, ranks, me_ref[0]):
        rows = span(r, seg)
        q_ref[rows, :] = slab[0]
        k_ref[rows, :] = slab[1]
        v_ref[rows, :] = slab[2]
    for r, slab in each_slab(g_ins, ranks, me_ref[0]):
        g_ref[span(r, seg), :] = slab[...]
    for t in range(total // tk):
        kt_ref[:, t * tk : (t + 1) * tk] = k_ref[t * tk : (t + 1) * tk, :].T
    nq = lax.div(length + (tq - 1), tq)
    nk = lax.div(length + (tk - 1), tk)
    dk_ref[...] = jnp.zeros_like(dk_ref)
    dv_ref[...] = jnp.zeros_like(dv_ref)

    def with_tiles(tiles):
        def q_step(i, _):
            q = q_ref[span(i, tq), :]
            g = g_ref[span(i, tq), :]
            offset = st_ref[0:1, span(i, tq)]
            delta = jnp.sum(
                ot_ref[:, span(i, tq)] * g.astype(jnp.float32).T, axis=0, keepdims=True
            )
            dq = jnp.zeros((HD, tq), jnp.float32)

            part = tk // 2
            parts = [slice(at, at + part) for at in range(0, tiles * tk, part)]

            def products(rows):
                return dot(k_ref[rows, :], q, NT), dot(v_ref[rows, :], g, NT)

            ahead = products(parts[0])
            for t, rows in enumerate(parts):
                s, dp = ahead
                if t + 1 < len(parts):
                    ahead = products(parts[t + 1])
                s = s * (SCALE * LOG2E) - offset
                if t + 2 >= len(parts):
                    row = lax.broadcasted_iota(jnp.int32, (part, tq), 0) + rows.start
                    s = jnp.where(row < length, s, NEG)
                p = jnp.exp2(s)
                ds = (p * (dp - delta)).astype(jnp.bfloat16)
                dv_ref[rows, :] += dot(p.astype(jnp.bfloat16), g, NN)
                dk_ref[rows, :] += dot(ds, q, NN)
                dq = dq + dot(kt_ref[:, rows], ds, NN)
            dq_ref[span(i, tq), :] = (dq.T * SCALE).astype(jnp.bfloat16)
            return 0

        lax.fori_loop(0, nq, q_step, 0)

    for_each_count(nk, total // tk, with_tiles)

    def blank(i, _):
        dq_ref[span(i, tq), :] = jnp.zeros((tq, HD), jnp.bfloat16)
        return 0

    lax.fori_loop(nq, total // tq, blank, 0)
    for r, slab in each_slab(outs, ranks, me_ref[0]):
        rows = span(r, seg)
        slab[0] = dq_ref[rows, :]
        slab[1] = (dk_ref[rows, :] * SCALE).astype(jnp.bfloat16)
        slab[2] = dv_ref[rows, :].astype(jnp.bfloat16)


def backward(qkv, g_in, kept, plan, ranks, where, deps):
    split = len(qkv) > 1
    per, seg = qkv[0].shape[-3:-1]
    heads = ranks * per // plan[2]
    total = ranks * seg
    tq, tk = tiles_of(total, seg)
    block = (3, None, seg, HD)
    return pl.pallas_call(
        functools.partial(backward_kernel, (len(qkv), len(deps), ranks, seg, tq, tk, plan, heads)),
        grid_spec=pltpu.PrefetchScalarGridSpec(
            num_scalar_prefetch=2,
            grid=(per,),
            in_specs=slab_specs(split, ranks, block, lambda p, n, m: (0, p, 0, 0))
            + slab_specs(split, ranks, (None, seg, HD), lambda p, n, m: (p, 0, 0))
            + [
                pl.BlockSpec((None, 8, total), lambda p, n, m: (p, 0, 0)),
                pl.BlockSpec((None, HD, total), lambda p, n, m: (p, 0, 0)),
            ]
            + unread(deps),
            out_specs=slab_specs(split, ranks, block, lambda p, n, m: (0, p, 0, 0)),
            scratch_shapes=[pltpu.VMEM((total, HD), jnp.bfloat16)] * 4
            + [
                pltpu.VMEM((HD, total), jnp.bfloat16),
                pltpu.VMEM((total, HD), jnp.bfloat16),
                pltpu.VMEM((total, HD), jnp.float32),
                pltpu.VMEM((total, HD), jnp.float32),
            ],
        ),
        out_shape=slab_shapes(split, ranks, (3, per, seg, HD)),
        cost_estimate=cost(20 * per * total * total * HD, 14 * per * total * HD, per * total * total),
        compiler_params=pltpu.CompilerParams(vmem_limit_bytes=VMEM_LIMIT),
        name="attend_bwd",
    )(*where, *qkv, *g_in, *kept, *deps)


def gather_rows(rows, deps):
    planes = lax.axis_size("grp") * lax.axis_size("dp")
    enc = rows.shape[1]
    shares = 1
    while shares * 2 <= planes and enc % (shares * 2 * HD) == 0:
        shares *= 2
    plane = lax.axis_index("grp") * lax.axis_size("dp") + lax.axis_index("dp")
    wide = enc // shares
    mine = lax.dynamic_slice_in_dim(rows, (plane % shares) * wide, wide, axis=1)
    along = after(lax.all_gather(mine, "seq", axis=0, tiled=True), deps)
    groups = [list(range(at, at + shares)) for at in range(0, planes, shares)]
    return lax.all_gather(
        along, ("grp", "dp"), axis=0, axis_index_groups=groups if len(groups) > 1 else None
    )


def norm_kernel(t_ref, gain_ref, bias_ref, _, out_ref):
    data = t_ref[...].astype(jnp.float32)
    center = data - jnp.mean(data, axis=-1, keepdims=True)
    spread = jnp.mean(center * center, axis=-1, keepdims=True)
    normed = center * lax.rsqrt(spread + EPS) * gain_ref[...] + bias_ref[...]
    out_ref[...] = normed.astype(jnp.bfloat16)


def layer_norm(rows, gain, bias, dep):
    count, seg, enc = rows.shape
    block = pl.BlockSpec((None, seg, enc), lambda b: (b, 0, 0))
    vector = pl.BlockSpec((1, enc), lambda b: (0, 0))
    return pl.pallas_call(
        norm_kernel,
        grid=(count,),
        in_specs=[block, vector, vector] + unread([dep]),
        out_specs=block,
        out_shape=jax.ShapeDtypeStruct(rows.shape, jnp.bfloat16),
        cost_estimate=cost(10 * rows.size, 4 * rows.size),
        compiler_params=pltpu.CompilerParams(vmem_limit_bytes=VMEM_LIMIT),
        name="layer_norm",
    )(rows, gain.reshape(1, -1), bias.reshape(1, -1), dep)


def after_kernel(*_):
    pass


def after(value, deps):
    return pl.pallas_call(
        after_kernel,
        in_specs=unread([value, *deps]),
        out_specs=pl.BlockSpec(memory_space=pl.ANY),
        out_shape=jax.ShapeDtypeStruct(value.shape, value.dtype),
        input_output_aliases={0: 0},
        cost_estimate=cost(0, 0),
        name="after",
    )(value, *deps)


def head_kernel(sizes, len_ref, me_ref, *refs):
    n_slabs, ranks, plan, per, seg = sizes
    images = plan[2]
    image = image_at(plan, len_ref, me_ref)
    ins = refs[:n_slabs]
    w_ref, t_ref = refs[n_slabs : n_slabs + 2]
    outs, rows_ref = refs[-1 - n_slabs : -1], refs[-1]
    heads = ranks * per // images

    def place_of(r, j):
        pair = r * per + j
        return span(lax.div(pair, heads), seg), span(lax.rem(pair, heads), HD)

    for r, slab in each_slab(ins, ranks, me_ref[0]):
        for j in range(per):
            rows, cols = place_of(jnp.int32(r), j)
            rows_ref[rows, cols] = slab[j]
    shares, _, wide = w_ref.shape
    for b in range(images):
        rows = rows_ref[b * seg : (b + 1) * seg, :]
        aligned = jnp.concatenate([dot(rows, w_ref[part], NN) for part in range(shares)], axis=1)
        tgt = t_ref[b].astype(jnp.float32)
        width = aligned.shape[-1]
        inner = jnp.mean(aligned * tgt, axis=-1, keepdims=True)
        own = jnp.mean(aligned * aligned, axis=-1, keepdims=True) + EPS
        other = jnp.mean(tgt * tgt, axis=-1, keepdims=True) + EPS
        inverse = lax.rsqrt(own * other)
        cosine = inner * inverse
        row = lax.broadcasted_iota(jnp.int32, (seg, 1), 0) + me_ref[1]
        keep = jnp.where(row < len_ref[me_ref[2] + image + b], -COEF / width, 0.0)
        grad = (keep * (tgt * inverse - cosine / own * aligned)).astype(jnp.bfloat16)
        grad_rows = dot(grad[:, :wide], w_ref[0], NT)
        for part in range(1, shares):
            grad_rows += dot(grad[:, part * wide : (part + 1) * wide], w_ref[part], NT)
        rows_ref[b * seg : (b + 1) * seg, :] = grad_rows.astype(jnp.bfloat16)
    for r, slab in each_slab(outs, ranks, me_ref[0]):
        for j in range(per):
            rows, cols = place_of(jnp.int32(r), j)
            slab[j] = rows_ref[rows, cols]


def align_head(back, whole, target, plan, ranks, where, deps):
    split = len(back) > 1
    per, seg = back[0].shape[-3:-1]
    shares, width, wide = whole.shape
    enc, images = shares * wide, plan[2]
    slabs = slab_specs(split, ranks, (per, seg, HD), lambda b, n, m: (0, 0, 0))
    return pl.pallas_call(
        functools.partial(head_kernel, (len(back), ranks, plan, per, seg)),
        grid_spec=pltpu.PrefetchScalarGridSpec(
            num_scalar_prefetch=2,
            grid=(1,),
            in_specs=slabs
            + [
                pl.BlockSpec((shares, width, wide), lambda b, n, m: (0, 0, 0)),
                pl.BlockSpec((images, seg, enc), lambda b, n, m: (lax.div(image_at(plan, n, m), images), 0, 0)),
            ]
            + unread(deps),
            out_specs=slabs,
            scratch_shapes=[pltpu.VMEM((images * seg, width), jnp.bfloat16)],
        ),
        out_shape=slab_shapes(split, ranks, (per, seg, HD)),
        cost_estimate=cost(
            4 * images * seg * width * enc, 2 * width * enc + 10 * images * seg * width, 0
        ),
        compiler_params=pltpu.CompilerParams(vmem_limit_bytes=VMEM_LIMIT),
        name="align_head",
    )(*where, *back, whole, target, *deps)


def shards(queries, key_states, value_states, projector, teacher, enc_gain, enc_bias, valid_len):
    ranks = lax.axis_size("seq")
    count, seg, width = queries.shape
    heads = width // HD
    images = 1
    while images * heads % ranks:
        images *= 2
    chunks = count // images
    per = images * heads // ranks
    rank = lax.axis_index("seq").astype(jnp.int32)

    first_image = (lax.axis_index("grp") * lax.axis_size("dp") + lax.axis_index("dp")) * count
    where = (valid_len, jnp.stack([rank, rank * seg, first_image.astype(jnp.int32)]))
    plans = [(c, chunks, images) for c in range(chunks)]
    split = [chunks > 1 and c == chunks - 1 for c in range(chunks)]

    arrays = (queries, key_states, value_states)
    packed = []
    for c in range(chunks):
        deps = [slabs[0] for slabs in packed]
        packed.append(pack(arrays, plans[c], ranks, per, split[c], where, deps))
    normed = layer_norm(teacher, enc_gain, enc_bias, packed[0][0])
    target = from_partner(normed, "grp", 0)
    whole = gather_rows(projector, packed[-1][:1])

    def ahead(near, made, c, also=[]):
        if not split[-1]:
            return []
        return made[c - 1][:1] if split[c] else near[-1][:3] + also

    qkv = [exchange(slabs) for slabs in packed]
    attended, kept = [], []
    for c in range(chunks):
        slabs, state = forward(qkv[c], plans[c], ranks, where, ahead(qkv, attended, c, [target]))
        kept.append(state)
        attended.append(slabs)
    back = [exchange(slabs) for slabs in attended]
    grad_rows = []
    for c in range(chunks):
        deps = ahead(back, grad_rows, c)
        grad_rows.append(align_head(back[c], whole, target, plans[c], ranks, where, deps))
    g_in = [exchange(slabs) for slabs in grad_rows]
    grads = []
    for c in range(chunks):
        deps = ahead(g_in, grads, c)
        grads.append(backward(qkv[c], g_in[c], kept[c], plans[c], ranks, where, deps))
    grads = [exchange(slabs) for slabs in grads]
    outs = ()
    for c in range(chunks):
        if not split[c]:
            outs = unpack(grads[c][0], plans[c], count, where, outs, ahead(grads, None, c))
            continue
        for s, slab in enumerate(grads[c]):
            outs = place(slab, s, plans[c], count, ranks, where, outs)
    return tuple(outs)


def solution(mesh):
    return jax.shard_map(
        shards,
        mesh=mesh,
        in_specs=(
            P(("grp", "dp"), "seq", None),
            P(("grp", "dp"), "seq", None),
            P(("grp", "dp"), "seq", None),
            P("seq", None),
            P(("grp", "dp"), "seq", None),
            P(),
            P(),
            P(),
        ),
        out_specs=(
            P(("grp", "dp"), "seq", None),
            P(("grp", "dp"), "seq", None),
            P(("grp", "dp"), "seq", None),
        ),
        check_vma=False,
    )
```

time: 887 us -> 434 us (0.49); the launches traced: 873 us -> 429 us
  matrix products: 294 us -> 0 us
  waiting for transfers between devices: 346 us -> 201 us
  Pallas kernels: 0 us -> 139 us
  local copies, waits for them, and re-layouts: 97 us -> 5.2 us
  other arithmetic: 61.3 us -> 0.58 us
    all_to_all x8 -> x4, waiting for transfers between devices: 309 us -> 8.8 us  [exchange(): lax.all_to_all(slabs[0], 'seq', split_axis=0, concat_axis=0, tiled=True)]
    dot_general x22 -> x0, matrix products: 212 us -> none  [the longest x4 62.4 us: backward_block(): jnp.einsum('pid,pjd->pij', g_part, vh, preferred_element_type=jnp.float32)]
    ppermute x0 -> x28, waiting for transfers between devices: none -> 165 us  [exchange(): lax.ppermute(slab, 'seq', [(i, i ^ s) for i in range(ranks)])]
    pallas_call x0 -> x19, Pallas kernels: none -> 139 us  [the longest x2 55.6 us: backward(): pl.pallas_call(functools.partial(backward_kernel, (len(qkv), len(deps), r...]
    sub x8 -> x0, matrix products: 82.7 us -> none  [the longest x4 43.6 us: backward_block(): grad_scores = (probs * (grad_probs - delta) * scale).astype(jnp.bfloat16)]
    dynamic_update_slice x4 -> x0, other arithmetic: 47.3 us -> none  [shards(): att_blocks, kept_probs = lax.map(forward_block, q_blocks)]
    unnamed x24 -> x36, local copies, waits for them, and re-layouts: 47 us -> 3.28 us
    ppermute x0 -> x28, starting transfers between devices: none -> 39.8 us  [exchange(): lax.ppermute(slab, 'seq', [(i, i ^ s) for i in range(ranks)])]
  transfers between devices with their start and end apart: 10 -> 35, of which waited for: 9 -> 15; matrix products, arithmetic and copies ran while one was open for 22% -> 0% of each run, Pallas kernels for 0% -> 31%
where the time goes in v1:
time: 434 us; the launch traced here: 429 us
  waiting for transfers between devices  201 us (46%)
  Pallas kernels  139 us (32%)
  starting transfers between devices  69.3 us (16%)
  between operations  14.5 us (3%)
  local copies, waits for them, and re-layouts  5.2 us (1%)
    ppermute x28, waiting for transfers between devices, exchange(): lax.ppermute(slab, 'seq', [(i, i ^ s) for i in range(ranks)])  165 us
    pallas_call x2, Pallas kernels, backward(): pl.pallas_call(functools.partial(backward_kernel, (len(qkv), len(deps), r...  55.6 us
    ppermute x28, starting transfers between devices, exchange(): lax.ppermute(slab, 'seq', [(i, i ^ s) for i in range(ranks)])  39.8 us
    pallas_call x2, Pallas kernels, forward(): pl.pallas_call(functools.partial(forward_kernel, (len(qkv), len(deps), ra...  29.5 us
    all_to_all x4, starting transfers between devices, exchange(): lax.all_to_all(slabs[0], 'seq', split_axis=0, concat_axis=0, tiled=True)  29.2 us
    all_gather x1, waiting for transfers between devices, gather_rows(): along = after(lax.all_gather(mine, 'seq', axis=0, tiled=True), deps)  26.8 us
    pallas_call x2, Pallas kernels, align_head(): pl.pallas_call(functools.partial(head_kernel, (len(back), ranks, plan, pe...  19.9 us
    pallas_call x8, Pallas kernels, place(): pl.pallas_call(functools.partial(place_kernel, per, parts), grid_spec=plt...  15.8 us
  transfers between devices with their start and end apart: 35, of which 15 were waited for; matrix products, arithmetic and copies ran while one was open for 0% of the time, Pallas kernels for 31%

profile of v1, /device:TPU:13, one launch (start us, length us, event | category | flops | bytes accessed | tf_op | source)
XLA Modules:
  0.0 429.4 jit_solution(17884220691927638851)
XLA Ops:
  7.8 5.1 %pack.2.refs_24_._ = bf16[8,3,2,256,128]{4,3,2,1,0:T(8,128)(2,1)} custom-call(s32[8]{0:T(128)} %_.21, s32[3]{0:T(128)} %pad_add_fusion.__.me_ref, bf16[2,256,2048]{2,1,0:T(8,128)(2,1)} %refs_21_.1, bf16[2,256,2048]{2,1,0:T(8,128)(2,1)} %refs_22_.1, bf16[2,256,2048]{2,1,0:T(8,128)(2,1)} %refs_23_.1), custom_call_target="tpu_custom_call" | custom-call | bytes 100663296 | tf_op jit(solution)/shard_map/pack/pallas_call | solution.py:141
  12.9 5.8 %all-to-all-start = ((bf16[8,3,2,256,128]{4,3,2,1,0:T(8,128)(2,1)}), bf16[8,3,2,256,128]{4,3,2,1,0:T(8,128)(2,1)}, u32[]{:S(2)}, u32[]{:S(2)}) async-start(bf16[8,3,2,256,128]{4,3,2,1,0:T(8,128)(2,1)} %pack.2.refs_24_._), calls=%async_computation | async-start | bytes 6291456 | tf_op jit(solution)/shard_map/all_to_all | solution.py:39
  20.7 3.2 layer_norm.1
  24.0 4.7 %pack.3 = (bf16[3,2,256,128]{3,2,1,0:T(8,128)(2,1)}, bf16[3,2,256,128]{3,2,1,0:T(8,128)(2,1)}, bf16[3,2,256,128]{3,2,1,0:T(8,128)(2,1)}, bf16[3,2,256,128]{3,2,1...) custom-call(s32[8]{0:T(128)} %_.21, ...), custom_call_target="tpu_custom_call" | custom-call | bytes 100663296 | tf_op jit(solution)/shard_map/pack/pallas_call | solution.py:141
  33.2 26.8 %all-gather.4.cloned.1.call-done.__0_ = bf16[2048,384]{1,0:T(8,128)(2,1)} async-done(((bf16[256,384]{1,0:T(8,128)(2,1)}), bf16[2048,384]{1,0:T(8,128)(2,1)}) %all-gather.4.cloned.1.call-update) | async-done | bytes 1572880 | tf_op jit(solution)/shard_map/all_gather | solution.py:467
  60.0 7.9 %collective-permute-start.4 = (bf16[3,2,256,128]{3,2,1,0:T(8,128)(2,1)}, bf16[3,2,256,128]{3,2,1,0:T(8,128)(2,1)}, u32[]{:S(2)}, u32[]{:S(2)}) collective-permute-start(bf16[3,2,256,128]{3,2,1,0:T(8,128)(2,1)} %get-tuple-element.69), channel_id=1, source_target_pairs={{0,10},{2,8},{4,14},{6,12},{8,2},{10,0},{12,6},{14,4},{1,11},{3,9}... | collective-permute-start | bytes 1179656 | tf_op jit(solution)/shard_map/ppermute | solution.py:42
  67.9 23.8 %collective-permute-done.1.refs_3_.refs_2_ = bf16[3,2,256,128]{3,2,1,0:T(8,128)(2,1)S(1)} collective-permute-done((bf16[3,2,256,128]{3,2,1,0:T(8,128)(2,1)}, bf16[3,2,256,128]{3,2,1,0:T(8,128)(2,1)S(1)}, u32[]{:S(2)}, u32[]{:S(2)}) %collective-permute-start.1) | collective-permute-done | bytes 393248 | tf_op jit(solution)/shard_map/ppermute | solution.py:42
  95.0 4.4 %all-to-all-done.refs_0_ = bf16[8,3,2,256,128]{4,3,2,1,0:T(8,128)(2,1)} async-done(((bf16[8,3,2,256,128]{4,3,2,1,0:T(8,128)(2,1)}), bf16[8,3,2,256,128]{4,3,2,1,0:T(8,128)(2,1)}, u32[]{:S(2)}, u32[]{:S(2)}) %all-to-all-start) | async-done | bytes 3145760 | tf_op jit(solution)/shard_map/all_to_all | solution.py:39
  99.4 14.4 %attend_fwd.2 = (bf16[8,2,256,128]{3,2,1,0:T(8,128)(2,1)}, f32[2,8,2048]{2,1,0:T(8,128)}, f32[2,128,2048]{2,1,0:T(8,128)}) custom-call(s32[8]{0:T(128)} %_.21, s32[3]{0:T(128)} %pad_add_fusion.__.me_ref, bf16[8,3,2,256,128]{4,3,2,1,0:T(8,128)(2,1)} %all-to-all-done.refs_0_, bf16[3,2,256,128]{3,2,1,0:T(8,128)(2,1)} %get-tuple-element.64.refs_1_.refs_0_.__1_, ...), custom_call_target="tpu_custom_call" | custom-call | flops 137438953472 | bytes 67108864 | tf_op jit(solution)/shard_map/attend_fwd/pallas_call | solution.py:319
  113.8 8.0 %all-to-all-start.1 = ((bf16[8,2,256,128]{3,2,1,0:T(8,128)(2,1)}), bf16[8,2,256,128]{3,2,1,0:T(8,128)(2,1)S(1)}, u32[]{:S(2)}, u32[]{:S(2)}) async-start(bf16[8,2,256,128]{3,2,1,0:T(8,128)(2,1)} %get-tuple-element.72.refs_8_), calls=%async_computation.1 | async-start | bytes 2097152 | tf_op jit(solution)/shard_map/all_to_all | solution.py:39
  121.8 30.9 %collective-permute-done.3.refs_4_ = bf16[3,2,256,128]{3,2,1,0:T(8,128)(2,1)} collective-permute-done((bf16[3,2,256,128]{3,2,1,0:T(8,128)(2,1)}, bf16[3,2,256,128]{3,2,1,0:T(8,128)(2,1)}, u32[]{:S(2)}, u32[]{:S(2)}) %collective-permute-start.3) | collective-permute-done | bytes 393248 | tf_op jit(solution)/shard_map/ppermute | solution.py:42
  152.7 8.4 %collective-permute-done.4.refs_5_ = bf16[3,2,256,128]{3,2,1,0:T(8,128)(2,1)} collective-permute-done((bf16[3,2,256,128]{3,2,1,0:T(8,128)(2,1)}, bf16[3,2,256,128]{3,2,1,0:T(8,128)(2,1)}, u32[]{:S(2)}, u32[]{:S(2)}) %collective-permute-start.4) | collective-permute-done | bytes 393248 | tf_op jit(solution)/shard_map/ppermute | solution.py:42
  161.1 10.1 %collective-permute-done.5.refs_6_ = bf16[3,2,256,128]{3,2,1,0:T(8,128)(2,1)} collective-permute-done((bf16[3,2,256,128]{3,2,1,0:T(8,128)(2,1)}, bf16[3,2,256,128]{3,2,1,0:T(8,128)(2,1)}, u32[]{:S(2)}, u32[]{:S(2)}) %collective-permute-start.5) | collective-permute-done | bytes 393248 | tf_op jit(solution)/shard_map/ppermute | solution.py:42
  171.2 9.1 %collective-permute-done.6.refs_7_ = bf16[3,2,256,128]{3,2,1,0:T(8,128)(2,1)} collective-permute-done((bf16[3,2,256,128]{3,2,1,0:T(8,128)(2,1)}, bf16[3,2,256,128]{3,2,1,0:T(8,128)(2,1)}, u32[]{:S(2)}, u32[]{:S(2)}) %collective-permute-start.6) | collective-permute-done | bytes 393248 | tf_op jit(solution)/shard_map/ppermute | solution.py:42
  180.3 15.0 %attend_fwd.3 = (bf16[2,256,128]{2,1,0:T(8,128)(2,1)}, bf16[2,256,128]{2,1,0:T(8,128)(2,1)}, bf16[2,256,128]{2,1,0:T(8,128)(2,1)}, bf16[2,256,128]{2,1,0:T(8,128...) custom-call(s32[8]{0:T(128)} %_.21, ...), custom_call_target="tpu_custom_call" | custom-call | flops 137438953472 | bytes 67108864 | tf_op jit(solution)/shard_map/attend_fwd/pallas_call | solution.py:319
  203.8 9.8 %align_head.2.refs_10_ = bf16[8,2,256,128]{3,2,1,0:T(8,128)(2,1)} custom-call(s32[8]{0:T(128)} %_.21, s32[3]{0:T(128)} %pad_add_fusion.__.me_ref, bf16[8,2,256,128]{3,2,1,0:T(8,128)(2,1)} %copy-done.9, bf16[4,2048,384]{2,1,0:T(8,128)(2,1)} %bitcast.4, bf16[2,256,1536]{2,1,0:T(8,128)(2,1)} %collective-permute-done.7.refs_4_.refs_2_.refs_9_, ...), custom_call_target="tpu_custom_call" | custom-call | flops 51539607552 | bytes 184549376 | tf_op jit(solution)/shard_map/align_head/pallas_call | solution.py:561
  213.6 8.8 %all-to-all-start.2 = ((bf16[8,2,256,128]{3,2,1,0:T(8,128)(2,1)}), bf16[8,2,256,128]{3,2,1,0:T(8,128)(2,1)S(1)}, u32[]{:S(2)}, u32[]{:S(2)}) async-start(bf16[8,2,256,128]{3,2,1,0:T(8,128)(2,1)} %align_head.2.refs_10_), calls=%async_computation.2 | async-start | bytes 2097152 | tf_op jit(solution)/shard_map/all_to_all | solution.py:39
  222.5 10.1 %align_head.3 = (bf16[2,256,128]{2,1,0:T(8,128)(2,1)}, bf16[2,256,128]{2,1,0:T(8,128)(2,1)}, bf16[2,256,128]{2,1,0:T(8,128)(2,1)}, bf16[2,256,128]{2,1,0:T(8,128...) custom-call(s32[8]{0:T(128)} %_.21, ...), custom_call_target="tpu_custom_call" | custom-call | flops 51539607552 | bytes 184549376 | tf_op jit(solution)/shard_map/align_head/pallas_call | solution.py:561
  238.6 4.9 %collective-permute-done.16.refs_6_.refs_10_ = bf16[2,256,128]{2,1,0:T(8,128)(2,1)S(1)} collective-permute-done((bf16[2,256,128]{2,1,0:T(8,128)(2,1)}, bf16[2,256,128]{2,1,0:T(8,128)(2,1)S(1)}, u32[]{:S(2)}, u32[]{:S(2)}) %collective-permute-start.16) | collective-permute-done | bytes 131104 | tf_op jit(solution)/shard_map/ppermute | solution.py:42
  244.1 3.3 collective-permute-start.21
  248.4 27.7 %attend_bwd.2.refs_18_ = bf16[8,3,2,256,128]{4,3,2,1,0:T(8,128)(2,1)} custom-call(s32[8]{0:T(128)} %_.21, s32[3]{0:T(128)} %pad_add_fusion.__.me_ref, bf16[8,3,2,256,128]{4,3,2,1,0:T(8,128)(2,1)} %all-to-all-done.refs_0_, bf16[8,2,256,128]{3,2,1,0:T(8,128)(2,1)} %copy-done.8, f32[2,8,2048]{2,1,0:T(8,128)} %get-tuple-element.91.refs_2_, ...), custom_call_target="tpu_custom_call" | custom-call | flops 343597383680 | bytes 117440512 | tf_op jit(solution)/shard_map/attend_bwd/pallas_call | solution.py:430
  276.1 6.7 %all-to-all-start.3 = ((bf16[8,3,2,256,128]{4,3,2,1,0:T(8,128)(2,1)}), bf16[8,3,2,256,128]{4,3,2,1,0:T(8,128)(2,1)}, u32[]{:S(2)}, u32[]{:S(2)}) async-start(bf16[8,3,2,256,128]{4,3,2,1,0:T(8,128)(2,1)} %attend_bwd.2.refs_18_), calls=%async_computation.3 | async-start | bytes 6291456 | tf_op jit(solution)/shard_map/all_to_all | solution.py:39
  282.9 27.8 %attend_bwd.3 = (bf16[3,2,256,128]{3,2,1,0:T(8,128)(2,1)}, bf16[3,2,256,128]{3,2,1,0:T(8,128)(2,1)}, bf16[3,2,256,128]{3,2,1,0:T(8,128)(2,1)}, bf16[3,2,256,128]...) custom-call(s32[8]{0:T(128)} %_.21, ...), custom_call_target="tpu_custom_call" | custom-call | flops 343597383680 | bytes 117440512 | tf_op jit(solution)/shard_map/attend_bwd/pallas_call | solution.py:430
  315.8 27.4 %collective-permute-done.27.refs_3_.src = bf16[3,2,256,128]{3,2,1,0:T(8,128)(2,1)S(1)} collective-permute-done((bf16[3,2,256,128]{3,2,1,0:T(8,128)(2,1)}, bf16[3,2,256,128]{3,2,1,0:T(8,128)(2,1)S(1)}, u32[]{:S(2)}, u32[]{:S(2)}) %collective-permute-start.27) | collective-permute-done | bytes 393248 | tf_op jit(solution)/shard_map/ppermute | solution.py:42
  346.4 4.4 %all-to-all-done.3.refs_0_ = bf16[8,3,2,256,128]{4,3,2,1,0:T(8,128)(2,1)} async-done(((bf16[8,3,2,256,128]{4,3,2,1,0:T(8,128)(2,1)}), bf16[8,3,2,256,128]{4,3,2,1,0:T(8,128)(2,1)}, u32[]{:S(2)}, u32[]{:S(2)}) %all-to-all-start.3) | async-done | bytes 3145760 | tf_op jit(solution)/shard_map/all_to_all | solution.py:39
  350.8 5.2 %unpack.1 = (bf16[2,256,2048]{2,1,0:T(8,128)(2,1)}, bf16[2,256,2048]{2,1,0:T(8,128)(2,1)}, bf16[2,256,2048]{2,1,0:T(8,128)(2,1)}) custom-call(s32[8]{0:T(128)} %_.21, s32[3]{0:T(128)} %pad_add_fusion.__.me_ref, bf16[8,3,2,256,128]{4,3,2,1,0:T(8,128)(2,1)} %all-to-all-done.3.refs_0_, bf16[3,2,256,128]{3,2,1,0:T(8,128)(2,1)} %get-tuple-element.100.refs_1_.src, ...), custom_call_target="tpu_custom_call" | custom-call | bytes 100663296 | tf_op jit(solution)/shard_map/unpack/pallas_call | solution.py:178
  360.2 2.4 place.11
  362.5 30.3 %collective-permute-done.25.src = bf16[3,2,256,128]{3,2,1,0:T(8,128)(2,1)} collective-permute-done((bf16[3,2,256,128]{3,2,1,0:T(8,128)(2,1)}, bf16[3,2,256,128]{3,2,1,0:T(8,128)(2,1)}, u32[]{:S(2)}, u32[]{:S(2)}) %collective-permute-start.25) | collective-permute-done | bytes 393248 | tf_op jit(solution)/shard_map/ppermute | solution.py:42
  395.2 6.1 %collective-permute-done.24.src = bf16[3,2,256,128]{3,2,1,0:T(8,128)(2,1)} collective-permute-done((bf16[3,2,256,128]{3,2,1,0:T(8,128)(2,1)}, bf16[3,2,256,128]{3,2,1,0:T(8,128)(2,1)}, u32[]{:S(2)}, u32[]{:S(2)}) %collective-permute-start.24) | collective-permute-done | bytes 393248 | tf_op jit(solution)/shard_map/ppermute | solution.py:42
  403.7 7.8 %collective-permute-done.23.src = bf16[3,2,256,128]{3,2,1,0:T(8,128)(2,1)} collective-permute-done((bf16[3,2,256,128]{3,2,1,0:T(8,128)(2,1)}, bf16[3,2,256,128]{3,2,1,0:T(8,128)(2,1)}, u32[]{:S(2)}, u32[]{:S(2)}) %collective-permute-start.23) | collective-permute-done | bytes 393248 | tf_op jit(solution)/shard_map/ppermute | solution.py:42
  411.4 2.3 place.14
  413.8 6.2 %collective-permute-done.22.src = bf16[3,2,256,128]{3,2,1,0:T(8,128)(2,1)} collective-permute-done((bf16[3,2,256,128]{3,2,1,0:T(8,128)(2,1)}, bf16[3,2,256,128]{3,2,1,0:T(8,128)(2,1)}, u32[]{:S(2)}, u32[]{:S(2)}) %collective-permute-start.22) | collective-permute-done | bytes 393248 | tf_op jit(solution)/shard_map/ppermute | solution.py:42
  (99 shorter events, 46.1 us)
Async XLA Ops:
  12.9 86.5 %all-to-all-start = ((bf16[8,3,2,256,128]{4,3,2,1,0:T(8,128)(2,1)}), bf16[8,3,2,256,128]{4,3,2,1,0:T(8,128)(2,1)}, u32[]{:S(2)}, u32[]{:S(2)}) async-start(bf16[8,3,2,256,128]{4,3,2,1,0:T(8,128)(2,1)} %pack.2.refs_24_._), calls=%async_computation | async-start | bytes 6291456 | tf_op jit(solution)/shard_map/all_to_all | solution.py:39
  18.6 41.3 %all-gather.4.cloned.1.call-start = ((), (), s32[]{:S(2)}) async-start(), calls=%async_computation.4 | async-start | bytes 1769472 | tf_op jit(solution)/shard_map/all_gather | solution.py:467
  19.4 183.5 %all-gather.6.cloned.1.call-start = ((), (), s32[]{:S(2)}) async-start(), calls=%async_computation.5 | async-start | bytes 7864320 | tf_op jit(solution)/shard_map/all_gather | solution.py:469
  23.8 70.0 %collective-permute-start.7 = (bf16[2,256,1536]{2,1,0:T(8,128)(2,1)}, bf16[2,256,1536]{2,1,0:T(8,128)(2,1)}, u32[]{:S(2)}, u32[]{:S(2)}) collective-permute-start(bf16[2,256,1536]{2,1,0:T(8,128)(2,1)} %layer_norm.1), channel_id=1, source_target_pairs={{0,16},{16,0},{1,17},{17,1},{2,18},{18,2},{3,19},{19,3},{4,20},{20... | collective-permute-start | bytes 4718600 | tf_op jit(solution)/shard_map/ppermute | solution.py:34
  28.7 31.3 %collective-permute-start = (bf16[3,2,256,128]{3,2,1,0:T(8,128)(2,1)}, bf16[3,2,256,128]{3,2,1,0:T(8,128)(2,1)S(1)}, u32[]{:S(2)}, u32[]{:S(2)}) collective-permute-start(bf16[3,2,256,128]{3,2,1,0:T(8,128)(2,1)} %get-tuple-element.65), channel_id=1, source_target_pairs={{0,2},{2,0},{4,6},{6,4},{8,10},{10,8},{12,14},{14,12},{1,3},{3,1},... | collective-permute-start | bytes 1179656 | tf_op jit(solution)/shard_map/ppermute | solution.py:42
  29.4 62.3 %collective-permute-start.1 = (bf16[3,2,256,128]{3,2,1,0:T(8,128)(2,1)}, bf16[3,2,256,128]{3,2,1,0:T(8,128)(2,1)S(1)}, u32[]{:S(2)}, u32[]{:S(2)}) collective-permute-start(bf16[3,2,256,128]{3,2,1,0:T(8,128)(2,1)} %get-tuple-element.66), channel_id=1, source_target_pairs={{0,4},{2,6},{4,0},{6,2},{8,12},{10,14},{12,8},{14,10},{1,5},{3,7},... | collective-permute-start | bytes 1179656 | tf_op jit(solution)/shard_map/ppermute | solution.py:42
  29.4 92.4 %collective-permute-start.2 = (bf16[3,2,256,128]{3,2,1,0:T(8,128)(2,1)}, bf16[3,2,256,128]{3,2,1,0:T(8,128)(2,1)}, u32[]{:S(2)}, u32[]{:S(2)}) collective-permute-start(bf16[3,2,256,128]{3,2,1,0:T(8,128)(2,1)} %get-tuple-element.67), channel_id=1, source_target_pairs={{0,6},{2,4},{4,2},{6,0},{8,14},{10,12},{12,10},{14,8},{1,7},{3,5},... | collective-permute-start | bytes 1179656 | tf_op jit(solution)/shard_map/ppermute | solution.py:42
  31.1 121.6 %collective-permute-start.3 = (bf16[3,2,256,128]{3,2,1,0:T(8,128)(2,1)}, bf16[3,2,256,128]{3,2,1,0:T(8,128)(2,1)}, u32[]{:S(2)}, u32[]{:S(2)}) collective-permute-start(bf16[3,2,256,128]{3,2,1,0:T(8,128)(2,1)} %get-tuple-element.68), channel_id=1, source_target_pairs={{0,8},{2,10},{4,12},{6,14},{8,0},{10,2},{12,4},{14,6},{1,9},{3,11}... | collective-permute-start | bytes 1179656 | tf_op jit(solution)/shard_map/ppermute | solution.py:42
  60.0 101.1 %collective-permute-start.4 = (bf16[3,2,256,128]{3,2,1,0:T(8,128)(2,1)}, bf16[3,2,256,128]{3,2,1,0:T(8,128)(2,1)}, u32[]{:S(2)}, u32[]{:S(2)}) collective-permute-start(bf16[3,2,256,128]{3,2,1,0:T(8,128)(2,1)} %get-tuple-element.69), channel_id=1, source_target_pairs={{0,10},{2,8},{4,14},{6,12},{8,2},{10,0},{12,6},{14,4},{1,11},{3,9}... | collective-permute-start | bytes 1179656 | tf_op jit(solution)/shard_map/ppermute | solution.py:42
  91.8 79.5 %collective-permute-start.5 = (bf16[3,2,256,128]{3,2,1,0:T(8,128)(2,1)}, bf16[3,2,256,128]{3,2,1,0:T(8,128)(2,1)}, u32[]{:S(2)}, u32[]{:S(2)}) collective-permute-start(bf16[3,2,256,128]{3,2,1,0:T(8,128)(2,1)} %get-tuple-element.70), channel_id=1, source_target_pairs={{0,12},{2,14},{4,8},{6,10},{8,4},{10,6},{12,0},{14,2},{1,13},{3,15... | collective-permute-start | bytes 1179656 | tf_op jit(solution)/shard_map/ppermute | solution.py:42
  93.8 86.5 %collective-permute-start.6 = (bf16[3,2,256,128]{3,2,1,0:T(8,128)(2,1)}, bf16[3,2,256,128]{3,2,1,0:T(8,128)(2,1)}, u32[]{:S(2)}, u32[]{:S(2)}) collective-permute-start(bf16[3,2,256,128]{3,2,1,0:T(8,128)(2,1)} %get-tuple-element.71), channel_id=1, source_target_pairs={{0,14},{2,12},{4,10},{6,8},{8,6},{10,4},{12,2},{14,0},{1,15},{3,13... | collective-permute-start | bytes 1179656 | tf_op jit(solution)/shard_map/ppermute | solution.py:42
  113.8 89.0 %all-to-all-start.1 = ((bf16[8,2,256,128]{3,2,1,0:T(8,128)(2,1)}), bf16[8,2,256,128]{3,2,1,0:T(8,128)(2,1)S(1)}, u32[]{:S(2)}, u32[]{:S(2)}) async-start(bf16[8,2,256,128]{3,2,1,0:T(8,128)(2,1)} %get-tuple-element.72.refs_8_), calls=%async_computation.1 | async-start | bytes 2097152 | tf_op jit(solution)/shard_map/all_to_all | solution.py:39
  195.5 26.9 %collective-permute-start.10 = (bf16[2,256,128]{2,1,0:T(8,128)(2,1)}, bf16[2,256,128]{2,1,0:T(8,128)(2,1)}, u32[]{:S(2)}, u32[]{:S(2)}) collective-permute-start(bf16[2,256,128]{2,1,0:T(8,128)(2,1)} %get-tuple-element.76), channel_id=1, source_target_pairs={{0,6},{2,4},{4,2},{6,0},{8,14},{10,12},{12,10},{14,8},{1,7},{3,5},... | collective-permute-start | bytes 393224 | tf_op jit(solution)/shard_map/ppermute | solution.py:42
  197.5 24.9 %collective-permute-start.11 = (bf16[2,256,128]{2,1,0:T(8,128)(2,1)}, bf16[2,256,128]{2,1,0:T(8,128)(2,1)}, u32[]{:S(2)}, u32[]{:S(2)}) collective-permute-start(bf16[2,256,128]{2,1,0:T(8,128)(2,1)} %get-tuple-element.77), channel_id=1, source_target_pairs={{0,8},{2,10},{4,12},{6,14},{8,0},{10,2},{12,4},{14,6},{1,9},{3,11}... | collective-permute-start | bytes 393224 | tf_op jit(solution)/shard_map/ppermute | solution.py:42
  197.5 24.9 %collective-permute-start.12 = (bf16[2,256,128]{2,1,0:T(8,128)(2,1)}, bf16[2,256,128]{2,1,0:T(8,128)(2,1)}, u32[]{:S(2)}, u32[]{:S(2)}) collective-permute-start(bf16[2,256,128]{2,1,0:T(8,128)(2,1)} %get-tuple-element.78), channel_id=1, source_target_pairs={{0,10},{2,8},{4,14},{6,12},{8,2},{10,0},{12,6},{14,4},{1,11},{3,9}... | collective-permute-start | bytes 393224 | tf_op jit(solution)/shard_map/ppermute | solution.py:42
  199.9 22.6 %collective-permute-start.13 = (bf16[2,256,128]{2,1,0:T(8,128)(2,1)}, bf16[2,256,128]{2,1,0:T(8,128)(2,1)}, u32[]{:S(2)}, u32[]{:S(2)}) collective-permute-start(bf16[2,256,128]{2,1,0:T(8,128)(2,1)} %get-tuple-element.79), channel_id=1, source_target_pairs={{0,12},{2,14},{4,8},{6,10},{8,4},{10,6},{12,0},{14,2},{1,13},{3,15... | collective-permute-start | bytes 393224 | tf_op jit(solution)/shard_map/ppermute | solution.py:42
  201.0 21.5 %collective-permute-start.14 = (bf16[2,256,128]{2,1,0:T(8,128)(2,1)}, bf16[2,256,128]{2,1,0:T(8,128)(2,1)}, u32[]{:S(2)}, u32[]{:S(2)}) collective-permute-start(bf16[2,256,128]{2,1,0:T(8,128)(2,1)} %get-tuple-element.80), channel_id=1, source_target_pairs={{0,14},{2,12},{4,10},{6,8},{8,6},{10,4},{12,2},{14,0},{1,15},{3,13... | collective-permute-start | bytes 393224 | tf_op jit(solution)/shard_map/ppermute | solution.py:42
  213.6 33.7 %all-to-all-start.2 = ((bf16[8,2,256,128]{3,2,1,0:T(8,128)(2,1)}), bf16[8,2,256,128]{3,2,1,0:T(8,128)(2,1)S(1)}, u32[]{:S(2)}, u32[]{:S(2)}) async-start(bf16[8,2,256,128]{3,2,1,0:T(8,128)(2,1)} %align_head.2.refs_10_), calls=%async_computation.2 | async-start | bytes 2097152 | tf_op jit(solution)/shard_map/all_to_all | solution.py:39
  233.0 10.5 %collective-permute-start.16 = (bf16[2,256,128]{2,1,0:T(8,128)(2,1)}, bf16[2,256,128]{2,1,0:T(8,128)(2,1)S(1)}, u32[]{:S(2)}, u32[]{:S(2)}) collective-permute-start(bf16[2,256,128]{2,1,0:T(8,128)(2,1)} %get-tuple-element.83), channel_id=1, source_target_pairs={{0,4},{2,6},{4,0},{6,2},{8,12},{10,14},{12,8},{14,10},{1,5},{3,7},... | collective-permute-start | bytes 393224 | tf_op jit(solution)/shard_map/ppermute | solution.py:42
  233.0 49.8 %collective-permute-start.17 = (bf16[2,256,128]{2,1,0:T(8,128)(2,1)}, bf16[2,256,128]{2,1,0:T(8,128)(2,1)}, u32[]{:S(2)}, u32[]{:S(2)}) collective-permute-start(bf16[2,256,128]{2,1,0:T(8,128)(2,1)} %get-tuple-element.84), channel_id=1, source_target_pairs={{0,6},{2,4},{4,2},{6,0},{8,14},{10,12},{12,10},{14,8},{1,7},{3,5},... | collective-permute-start | bytes 393224 | tf_op jit(solution)/shard_map/ppermute | solution.py:42
  234.8 48.1 %collective-permute-start.18 = (bf16[2,256,128]{2,1,0:T(8,128)(2,1)}, bf16[2,256,128]{2,1,0:T(8,128)(2,1)}, u32[]{:S(2)}, u32[]{:S(2)}) collective-permute-start(bf16[2,256,128]{2,1,0:T(8,128)(2,1)} %get-tuple-element.85), channel_id=1, source_target_pairs={{0,8},{2,10},{4,12},{6,14},{8,0},{10,2},{12,4},{14,6},{1,9},{3,11}... | collective-permute-start | bytes 393224 | tf_op jit(solution)/shard_map/ppermute | solution.py:42
  236.8 46.0 %collective-permute-start.19 = (bf16[2,256,128]{2,1,0:T(8,128)(2,1)}, bf16[2,256,128]{2,1,0:T(8,128)(2,1)}, u32[]{:S(2)}, u32[]{:S(2)}) collective-permute-start(bf16[2,256,128]{2,1,0:T(8,128)(2,1)} %get-tuple-element.86), channel_id=1, source_target_pairs={{0,10},{2,8},{4,14},{6,12},{8,2},{10,0},{12,6},{14,4},{1,11},{3,9}... | collective-permute-start | bytes 393224 | tf_op jit(solution)/shard_map/ppermute | solution.py:42
  237.4 45.5 %collective-permute-start.20 = (bf16[2,256,128]{2,1,0:T(8,128)(2,1)}, bf16[2,256,128]{2,1,0:T(8,128)(2,1)}, u32[]{:S(2)}, u32[]{:S(2)}) collective-permute-start(bf16[2,256,128]{2,1,0:T(8,128)(2,1)} %get-tuple-element.87), channel_id=1, source_target_pairs={{0,12},{2,14},{4,8},{6,10},{8,4},{10,6},{12,0},{14,2},{1,13},{3,15... | collective-permute-start | bytes 393224 | tf_op jit(solution)/shard_map/ppermute | solution.py:42
  244.1 38.7 %collective-permute-start.21 = (bf16[2,256,128]{2,1,0:T(8,128)(2,1)}, bf16[2,256,128]{2,1,0:T(8,128)(2,1)}, u32[]{:S(2)}, u32[]{:S(2)}) collective-permute-start(bf16[2,256,128]{2,1,0:T(8,128)(2,1)} %get-tuple-element.88), channel_id=1, source_target_pairs={{0,14},{2,12},{4,10},{6,8},{8,6},{10,4},{12,2},{14,0},{1,15},{3,13... | collective-permute-start | bytes 393224 | tf_op jit(solution)/shard_map/ppermute | solution.py:42
  276.1 74.8 %all-to-all-start.3 = ((bf16[8,3,2,256,128]{4,3,2,1,0:T(8,128)(2,1)}), bf16[8,3,2,256,128]{4,3,2,1,0:T(8,128)(2,1)}, u32[]{:S(2)}, u32[]{:S(2)}) async-start(bf16[8,3,2,256,128]{4,3,2,1,0:T(8,128)(2,1)} %attend_bwd.2.refs_18_), calls=%async_computation.3 | async-start | bytes 6291456 | tf_op jit(solution)/shard_map/all_to_all | solution.py:39
  310.7 32.5 %collective-permute-start.27 = (bf16[3,2,256,128]{3,2,1,0:T(8,128)(2,1)}, bf16[3,2,256,128]{3,2,1,0:T(8,128)(2,1)S(1)}, u32[]{:S(2)}, u32[]{:S(2)}) collective-permute-start(bf16[3,2,256,128]{3,2,1,0:T(8,128)(2,1)} %get-tuple-element.98), channel_id=1, source_target_pairs={{0,4},{2,6},{4,0},{6,2},{8,12},{10,14},{12,8},{14,10},{1,5},{3,7},... | collective-permute-start | bytes 1179656 | tf_op jit(solution)/shard_map/ppermute | solution.py:42
  310.8 34.3 %collective-permute-start.28 = (bf16[3,2,256,128]{3,2,1,0:T(8,128)(2,1)}, bf16[3,2,256,128]{3,2,1,0:T(8,128)(2,1)S(1)}, u32[]{:S(2)}, u32[]{:S(2)}) collective-permute-start(bf16[3,2,256,128]{3,2,1,0:T(8,128)(2,1)} %get-tuple-element.99), channel_id=1, source_target_pairs={{0,2},{2,0},{4,6},{6,4},{8,10},{10,8},{12,14},{14,12},{1,3},{3,1},... | collective-permute-start | bytes 1179656 | tf_op jit(solution)/shard_map/ppermute | solution.py:42
  311.2 49.0 %collective-permute-start.26 = (bf16[3,2,256,128]{3,2,1,0:T(8,128)(2,1)}, bf16[3,2,256,128]{3,2,1,0:T(8,128)(2,1)}, u32[]{:S(2)}, u32[]{:S(2)}) collective-permute-start(bf16[3,2,256,128]{3,2,1,0:T(8,128)(2,1)} %get-tuple-element.97), channel_id=1, source_target_pairs={{0,6},{2,4},{4,2},{6,0},{8,14},{10,12},{12,10},{14,8},{1,7},{3,5},... | collective-permute-start | bytes 1179656 | tf_op jit(solution)/shard_map/ppermute | solution.py:42
  312.8 80.1 %collective-permute-start.25 = (bf16[3,2,256,128]{3,2,1,0:T(8,128)(2,1)}, bf16[3,2,256,128]{3,2,1,0:T(8,128)(2,1)}, u32[]{:S(2)}, u32[]{:S(2)}) collective-permute-start(bf16[3,2,256,128]{3,2,1,0:T(8,128)(2,1)} %get-tuple-element.96), channel_id=1, source_target_pairs={{0,8},{2,10},{4,12},{6,14},{8,0},{10,2},{12,4},{14,6},{1,9},{3,11}... | collective-permute-start | bytes 1179656 | tf_op jit(solution)/shard_map/ppermute | solution.py:42
  314.9 86.5 %collective-permute-start.24 = (bf16[3,2,256,128]{3,2,1,0:T(8,128)(2,1)}, bf16[3,2,256,128]{3,2,1,0:T(8,128)(2,1)}, u32[]{:S(2)}, u32[]{:S(2)}) collective-permute-start(bf16[3,2,256,128]{3,2,1,0:T(8,128)(2,1)} %get-tuple-element.95), channel_id=1, source_target_pairs={{0,10},{2,8},{4,14},{6,12},{8,2},{10,0},{12,6},{14,4},{1,11},{3,9}... | collective-permute-start | bytes 1179656 | tf_op jit(solution)/shard_map/ppermute | solution.py:42
  343.2 68.2 %collective-permute-start.23 = (bf16[3,2,256,128]{3,2,1,0:T(8,128)(2,1)}, bf16[3,2,256,128]{3,2,1,0:T(8,128)(2,1)}, u32[]{:S(2)}, u32[]{:S(2)}) collective-permute-start(bf16[3,2,256,128]{3,2,1,0:T(8,128)(2,1)} %get-tuple-element.94), channel_id=1, source_target_pairs={{0,12},{2,14},{4,8},{6,10},{8,4},{10,6},{12,0},{14,2},{1,13},{3,15... | collective-permute-start | bytes 1179656 | tf_op jit(solution)/shard_map/ppermute | solution.py:42
  345.2 74.9 %collective-permute-start.22 = (bf16[3,2,256,128]{3,2,1,0:T(8,128)(2,1)}, bf16[3,2,256,128]{3,2,1,0:T(8,128)(2,1)}, u32[]{:S(2)}, u32[]{:S(2)}) collective-permute-start(bf16[3,2,256,128]{3,2,1,0:T(8,128)(2,1)} %get-tuple-element.93), channel_id=1, source_target_pairs={{0,14},{2,12},{4,10},{6,8},{8,6},{10,4},{12,2},{14,0},{1,15},{3,13... | collective-permute-start | bytes 1179656 | tf_op jit(solution)/shard_map/ppermute | solution.py:42
  (21 other events, 134.4 us)
Sparse Core Ops, SparseCore 0:
  21.1 38.8 all-gather.3
  61.8 76.1 all-gather.5

commit v2 on v1

--- a/solution.py
+++ b/solution.py
@@ -348,13 +348,69 @@
     return attended, (stats, kept)
 
 
+def weights_kernel(sizes, len_ref, me_ref, *refs):
+    n_slabs, ranks, seg, tq, tk, plan, heads, per = sizes
+    ins, st_ref, p_ref = refs[:n_slabs], refs[n_slabs], refs[n_slabs + 1]
+    q_ref, k_ref = refs[n_slabs + 2 :]
+    i = pl.program_id(1)
+    pair = me_ref[0] * per + pl.program_id(0)
+    length = len_ref[me_ref[2] + image_at(plan, len_ref, me_ref) + lax.div(pair, heads)]
+
+    @pl.when(i == 0)
+    def _():
+        for r, slab in each_slab(ins, ranks, me_ref[0]):
+            q_ref[span(r, seg), :] = slab[0]
+            k_ref[span(r, seg), :] = slab[1]
+
+    @pl.when(i * tq < length)
+    def _():
+        q = q_ref[span(i, tq), :]
+        for t in range(ranks * seg // tk):
+            rows = slice(t * tk, (t + 1) * tk)
+            s = dot(k_ref[rows, :], q, NT) * (SCALE * LOG2E) - st_ref[0:1, :]
+            row = lax.broadcasted_iota(jnp.int32, (tk, tq), 0) + t * tk
+            p_ref[rows, :] = jnp.exp2(jnp.where(row < length, s, NEG)).astype(jnp.bfloat16)
+
+
+def weights(qkv, stats, plan, ranks, where):
+    split = len(qkv) > 1
+    per, seg = qkv[0].shape[-3:-1]
+    heads = ranks * per // plan[2]
+    total = ranks * seg
+    tq, tk = tiles_of(total, seg)
+    return pl.pallas_call(
+        functools.partial(weights_kernel, (len(qkv), ranks, seg, tq, tk, plan, heads, per)),
+        grid_spec=pltpu.PrefetchScalarGridSpec(
+            num_scalar_prefetch=2,
+            grid=(per, total // tq),
+            in_specs=slab_specs(split, ranks, (3, None, seg, HD), lambda p, i, n, m: (0, p, 0, 0))
+            + [pl.BlockSpec((None, 8, tq), lambda p, i, n, m: (p, 0, i))],
+            out_specs=pl.BlockSpec((None, total, tq), lambda p, i, n, m: (p, 0, i)),
+            scratch_shapes=[pltpu.VMEM((total, HD), jnp.bfloat16)] * 2,
+        ),
+        out_shape=jax.ShapeDtypeStruct((per, total, total), jnp.bfloat16),
+        cost_estimate=cost(2 * per * total * total * HD, 2 * per * total * total),
+        compiler_params=pltpu.CompilerParams(vmem_limit_bytes=VMEM_LIMIT),
+        name="weights",
+    )(*where, *qkv, stats)
+
+
 def backward_kernel(sizes, len_ref, me_ref, *refs):
-    n_slabs, n_deps, ranks, seg, tq, tk, plan, heads = sizes
+    n_slabs, n_deps, n_weights, ranks, seg, tq, tk, plan, heads = sizes
     ins, g_ins = refs[:n_slabs], refs[n_slabs : 2 * n_slabs]
-    st_ref, ot_ref = refs[2 * n_slabs : 2 * n_slabs + 2]
-    refs = refs[2 * n_slabs + 2 + n_deps :]
+    n_kept = 3 if n_weights else 2
+    st_ref, ot_ref, *w_ref = refs[2 * n_slabs : 2 * n_slabs + n_kept]
+    refs = refs[2 * n_slabs + n_kept + n_deps :]
     outs = refs[:n_slabs]
-    q_ref, k_ref, v_ref, g_ref, kt_ref, dq_ref, dk_ref, dv_ref = refs[n_slabs:]
+    q_ref, k_ref, v_ref, g_ref, kt_ref, dq_ref, dk_ref, dv_ref, *buf = refs[n_slabs:]
+
+    def fetch(i, slot):
+        buf_ref, sems = buf
+        source = w_ref[0].at[pl.program_id(0), :, span(i, tq)]
+        return pltpu.make_async_copy(source, buf_ref.at[slot], sems.at[slot])
+
+    if n_weights:
+        fetch(0, 0).start()
     length = pair_length(len_ref, me_ref, plan, heads)
     total = ranks * seg
     for r, slab in each_slab(ins, ranks, me_ref[0]):
@@ -384,19 +440,34 @@
             part = tk // 2
             parts = [slice(at, at + part) for at in range(0, tiles * tk, part)]
 
+            if n_weights:
+                slot = lax.rem(i, 2)
+
+                @pl.when(i + 1 < nq)
+                def _():
+                    fetch(i + 1, 1 - slot).start()
+
+                fetch(i, slot).wait()
+
             def products(rows):
-                return dot(k_ref[rows, :], q, NT), dot(v_ref[rows, :], g, NT)
+                dp = dot(v_ref[rows, :], g, NT)
+                if n_weights:
+                    return buf[0][slot, rows, :], dp
+                return dot(k_ref[rows, :], q, NT), dp
 
             ahead = products(parts[0])
             for t, rows in enumerate(parts):
                 s, dp = ahead
                 if t + 1 < len(parts):
                     ahead = products(parts[t + 1])
-                s = s * (SCALE * LOG2E) - offset
-                if t + 2 >= len(parts):
-                    row = lax.broadcasted_iota(jnp.int32, (part, tq), 0) + rows.start
-                    s = jnp.where(row < length, s, NEG)
-                p = jnp.exp2(s)
+                if n_weights:
+                    p = s.astype(jnp.float32)
+                else:
+                    s = s * (SCALE * LOG2E) - offset
+                    if t + 2 >= len(parts):
+                        row = lax.broadcasted_iota(jnp.int32, (part, tq), 0) + rows.start
+                        s = jnp.where(row < length, s, NEG)
+                    p = jnp.exp2(s)
                 ds = (p * (dp - delta)).astype(jnp.bfloat16)
                 dv_ref[rows, :] += dot(p.astype(jnp.bfloat16), g, NN)
                 dk_ref[rows, :] += dot(ds, q, NN)
@@ -420,15 +491,16 @@
         slab[2] = dv_ref[rows, :].astype(jnp.bfloat16)
 
 
-def backward(qkv, g_in, kept, plan, ranks, where, deps):
+def backward(qkv, g_in, kept, probs, plan, ranks, where, deps):
     split = len(qkv) > 1
     per, seg = qkv[0].shape[-3:-1]
     heads = ranks * per // plan[2]
     total = ranks * seg
     tq, tk = tiles_of(total, seg)
     block = (3, None, seg, HD)
+    held = [] if probs is None else [probs]
     return pl.pallas_call(
-        functools.partial(backward_kernel, (len(qkv), len(deps), ranks, seg, tq, tk, plan, heads)),
+        functools.partial(backward_kernel, (len(qkv), len(deps), len(held), ranks, seg, tq, tk, plan, heads)),
         grid_spec=pltpu.PrefetchScalarGridSpec(
             num_scalar_prefetch=2,
             grid=(per,),
@@ -438,6 +510,7 @@
                 pl.BlockSpec((None, 8, total), lambda p, n, m: (p, 0, 0)),
                 pl.BlockSpec((None, HD, total), lambda p, n, m: (p, 0, 0)),
             ]
+            + unread(held)
             + unread(deps),
             out_specs=slab_specs(split, ranks, block, lambda p, n, m: (0, p, 0, 0)),
             scratch_shapes=[pltpu.VMEM((total, HD), jnp.bfloat16)] * 4
@@ -446,13 +519,14 @@
                 pltpu.VMEM((total, HD), jnp.bfloat16),
                 pltpu.VMEM((total, HD), jnp.float32),
                 pltpu.VMEM((total, HD), jnp.float32),
-            ],
+            ]
+            + [pltpu.VMEM((2, total, tq), jnp.bfloat16), pltpu.SemaphoreType.DMA((2,))] * len(held),
         ),
         out_shape=slab_shapes(split, ranks, (3, per, seg, HD)),
         cost_estimate=cost(20 * per * total * total * HD, 14 * per * total * HD, per * total * total),
         compiler_params=pltpu.CompilerParams(vmem_limit_bytes=VMEM_LIMIT),
         name="attend_bwd",
-    )(*where, *qkv, *g_in, *kept, *deps)
+    )(*where, *qkv, *g_in, *kept, *held, *deps)
 
 
 def gather_rows(rows, deps):
@@ -613,8 +687,13 @@
 
     qkv = [exchange(slabs) for slabs in packed]
     attended, kept = [], []
+    probs = [None] * chunks
     for c in range(chunks):
-        slabs, state = forward(qkv[c], plans[c], ranks, where, ahead(qkv, attended, c, [target]))
+        deps = ahead(qkv, attended, c, [target])
+        if c and split[c]:
+            probs[c - 1] = weights(qkv[c - 1], kept[c - 1][0], plans[c - 1], ranks, where)
+            deps = list(deps) + [probs[c - 1]]
+        slabs, state = forward(qkv[c], plans[c], ranks, where, deps)
         kept.append(state)
         attended.append(slabs)
     back = [exchange(slabs) for slabs in attended]
@@ -626,7 +705,7 @@
     grads = []
     for c in range(chunks):
         deps = ahead(g_in, grads, c)
-        grads.append(backward(qkv[c], g_in[c], kept[c], plans[c], ranks, where, deps))
+        grads.append(backward(qkv[c], g_in[c], kept[c], probs[c], plans[c], ranks, where, deps))
     grads = [exchange(slabs) for slabs in grads]
     outs = ()
     for c in range(chunks):

time: 434 us -> 439 us (1.012)
  waiting for transfers between devices: 201 us -> 185 us
  Pallas kernels: 139 us -> 151 us
  starting transfers between devices: 69.3 us -> 79 us
    ppermute x28, waiting for transfers between devices: 165 us -> 149 us  [exchange(): lax.ppermute(slab, 'seq', [(i, i ^ s) for i in range(ranks)])]
    pallas_call x2 -> x3, Pallas kernels: 55.6 us -> 69.5 us  [the longest x2 55.7 us: backward(): pl.pallas_call(functools.partial(backward_kernel, (len(qkv), len(deps), l...]
    all_to_all x4, starting transfers between devices: 29.2 us -> 39 us  [exchange(): lax.all_to_all(slabs[0], 'seq', split_axis=0, concat_axis=0, tiled=True)]
  transfers between devices with their start and end apart: 35 -> 35, of which waited for: 15 -> 15; matrix products, arithmetic and copies ran while one was open for 0% -> 0% of each run, Pallas kernels for 31% -> 33%
where the time goes in v2:
time: 439 us; the launch traced here: 434 us
  waiting for transfers between devices  185 us (42%)
  Pallas kernels  151 us (34%)
  starting transfers between devices  79 us (18%)
  between operations  14.6 us (3%)
    ppermute x28, waiting for transfers between devices, exchange(): lax.ppermute(slab, 'seq', [(i, i ^ s) for i in range(ranks)])  149 us
    pallas_call x2, Pallas kernels, backward(): pl.pallas_call(functools.partial(backward_kernel, (len(qkv), len(deps), l...  55.7 us
    ppermute x28, starting transfers between devices, exchange(): lax.ppermute(slab, 'seq', [(i, i ^ s) for i in range(ranks)])  39.7 us
    all_to_all x4, starting transfers between devices, exchange(): lax.all_to_all(slabs[0], 'seq', split_axis=0, concat_axis=0, tiled=True)  39 us
    pallas_call x2, Pallas kernels, forward(): pl.pallas_call(functools.partial(forward_kernel, (len(qkv), len(deps), ra...  29.1 us
    all_gather x1, waiting for transfers between devices, gather_rows(): along = after(lax.all_gather(mine, 'seq', axis=0, tiled=True), deps)  26.8 us
    pallas_call x2, Pallas kernels, align_head(): pl.pallas_call(functools.partial(head_kernel, (len(back), ranks, plan, pe...  20 us
    pallas_call x8, Pallas kernels, place(): pl.pallas_call(functools.partial(place_kernel, per, parts), grid_spec=plt...  13.9 us
  transfers between devices with their start and end apart: 35, of which 15 were waited for; matrix products, arithmetic and copies ran while one was open for 0% of the time, Pallas kernels for 33%

profile of v2, /device:TPU:13, one launch (start us, length us, event | category | flops | bytes accessed | tf_op | source)
XLA Modules:
  0.0 433.6 jit_solution(3014029957088046972)
XLA Ops:
  7.8 5.1 %pack.2.refs_24_._ = bf16[8,3,2,256,128]{4,3,2,1,0:T(8,128)(2,1)} custom-call(s32[8]{0:T(128)} %_.21, s32[3]{0:T(128)} %pad_add_fusion.__.me_ref, bf16[2,256,2048]{2,1,0:T(8,128)(2,1)} %refs_21_.1, bf16[2,256,2048]{2,1,0:T(8,128)(2,1)} %refs_22_.1, bf16[2,256,2048]{2,1,0:T(8,128)(2,1)} %refs_23_.1), custom_call_target="tpu_custom_call" | custom-call | bytes 100663296 | tf_op jit(solution)/shard_map/pack/pallas_call | solution.py:141
  12.8 5.8 %all-to-all-start = ((bf16[8,3,2,256,128]{4,3,2,1,0:T(8,128)(2,1)}), bf16[8,3,2,256,128]{4,3,2,1,0:T(8,128)(2,1)}, u32[]{:S(2)}, u32[]{:S(2)}) async-start(bf16[8,3,2,256,128]{4,3,2,1,0:T(8,128)(2,1)} %pack.2.refs_24_._), calls=%async_computation | async-start | bytes 6291456 | tf_op jit(solution)/shard_map/all_to_all | solution.py:39
  20.6 3.2 layer_norm.1
  24.0 4.7 %pack.3 = (bf16[3,2,256,128]{3,2,1,0:T(8,128)(2,1)}, bf16[3,2,256,128]{3,2,1,0:T(8,128)(2,1)}, bf16[3,2,256,128]{3,2,1,0:T(8,128)(2,1)}, bf16[3,2,256,128]{3,2,1...) custom-call(s32[8]{0:T(128)} %_.21, ...), custom_call_target="tpu_custom_call" | custom-call | bytes 100663296 | tf_op jit(solution)/shard_map/pack/pallas_call | solution.py:141
  33.2 26.8 %all-gather.4.cloned.1.call-done.__0_ = bf16[2048,384]{1,0:T(8,128)(2,1)} async-done(((bf16[256,384]{1,0:T(8,128)(2,1)}), bf16[2048,384]{1,0:T(8,128)(2,1)}) %all-gather.4.cloned.1.call-update) | async-done | bytes 1572880 | tf_op jit(solution)/shard_map/all_gather | solution.py:541
  60.0 7.9 %collective-permute-start.4 = (bf16[3,2,256,128]{3,2,1,0:T(8,128)(2,1)}, bf16[3,2,256,128]{3,2,1,0:T(8,128)(2,1)}, u32[]{:S(2)}, u32[]{:S(2)}) collective-permute-start(bf16[3,2,256,128]{3,2,1,0:T(8,128)(2,1)} %get-tuple-element.69), channel_id=1, source_target_pairs={{0,10},{2,8},{4,14},{6,12},{8,2},{10,0},{12,6},{14,4},{1,11},{3,9}... | collective-permute-start | bytes 1179656 | tf_op jit(solution)/shard_map/ppermute | solution.py:42
  67.9 23.8 %collective-permute-done.1.refs_3_.refs_2_ = bf16[3,2,256,128]{3,2,1,0:T(8,128)(2,1)S(1)} collective-permute-done((bf16[3,2,256,128]{3,2,1,0:T(8,128)(2,1)}, bf16[3,2,256,128]{3,2,1,0:T(8,128)(2,1)S(1)}, u32[]{:S(2)}, u32[]{:S(2)}) %collective-permute-start.1) | collective-permute-done | bytes 393248 | tf_op jit(solution)/shard_map/ppermute | solution.py:42
  94.9 4.4 %all-to-all-done.refs_0_ = bf16[8,3,2,256,128]{4,3,2,1,0:T(8,128)(2,1)} async-done(((bf16[8,3,2,256,128]{4,3,2,1,0:T(8,128)(2,1)}), bf16[8,3,2,256,128]{4,3,2,1,0:T(8,128)(2,1)}, u32[]{:S(2)}, u32[]{:S(2)}) %all-to-all-start) | async-done | bytes 3145760 | tf_op jit(solution)/shard_map/all_to_all | solution.py:39
  99.4 14.4 %attend_fwd.2 = (bf16[8,2,256,128]{3,2,1,0:T(8,128)(2,1)}, f32[2,8,2048]{2,1,0:T(8,128)}, f32[2,128,2048]{2,1,0:T(8,128)}) custom-call(s32[8]{0:T(128)} %_.21, s32[3]{0:T(128)} %pad_add_fusion.__.me_ref, bf16[8,3,2,256,128]{4,3,2,1,0:T(8,128)(2,1)} %all-to-all-done.refs_0_, bf16[3,2,256,128]{3,2,1,0:T(8,128)(2,1)} %get-tuple-element.64.refs_1_.refs_0_.__1_, ...), custom_call_target="tpu_custom_call" | custom-call | flops 137438953472 | bytes 67108864 | tf_op jit(solution)/shard_map/attend_fwd/pallas_call | solution.py:319
  113.8 8.7 %all-to-all-start.1 = ((bf16[8,2,256,128]{3,2,1,0:T(8,128)(2,1)}), bf16[8,2,256,128]{3,2,1,0:T(8,128)(2,1)}, u32[]{:S(2)}, u32[]{:S(2)}) async-start(bf16[8,2,256,128]{3,2,1,0:T(8,128)(2,1)} %get-tuple-element.72.refs_8_), calls=%async_computation.1 | async-start | bytes 2097152 | tf_op jit(solution)/shard_map/all_to_all | solution.py:39
  122.5 13.8 %weights.1.refs_9_.refs_4_ = bf16[2,2048,2048]{2,1,0:T(8,128)(2,1)} custom-call(s32[8]{0:T(128)} %_.21, s32[3]{0:T(128)} %pad_add_fusion.__.me_ref, bf16[8,3,2,256,128]{4,3,2,1,0:T(8,128)(2,1)} %all-to-all-done.refs_0_, f32[2,8,2048]{2,1,0:T(8,128)} %get-tuple-element.73.refs_1_.refs_2_), custom_call_target="tpu_custom_call" | custom-call | flops 34359738368 | bytes 268435456 | tf_op jit(solution)/shard_map/weights/pallas_call | solution.py:381
  136.3 16.4 %collective-permute-done.3.refs_4_ = bf16[3,2,256,128]{3,2,1,0:T(8,128)(2,1)} collective-permute-done((bf16[3,2,256,128]{3,2,1,0:T(8,128)(2,1)}, bf16[3,2,256,128]{3,2,1,0:T(8,128)(2,1)}, u32[]{:S(2)}, u32[]{:S(2)}) %collective-permute-start.3) | collective-permute-done | bytes 393248 | tf_op jit(solution)/shard_map/ppermute | solution.py:42
  152.7 8.4 %collective-permute-done.4.refs_5_ = bf16[3,2,256,128]{3,2,1,0:T(8,128)(2,1)} collective-permute-done((bf16[3,2,256,128]{3,2,1,0:T(8,128)(2,1)}, bf16[3,2,256,128]{3,2,1,0:T(8,128)(2,1)}, u32[]{:S(2)}, u32[]{:S(2)}) %collective-permute-start.4) | collective-permute-done | bytes 393248 | tf_op jit(solution)/shard_map/ppermute | solution.py:42
  161.1 10.1 %collective-permute-done.5.refs_6_ = bf16[3,2,256,128]{3,2,1,0:T(8,128)(2,1)} collective-permute-done((bf16[3,2,256,128]{3,2,1,0:T(8,128)(2,1)}, bf16[3,2,256,128]{3,2,1,0:T(8,128)(2,1)}, u32[]{:S(2)}, u32[]{:S(2)}) %collective-permute-start.5) | collective-permute-done | bytes 393248 | tf_op jit(solution)/shard_map/ppermute | solution.py:42
  171.2 9.1 %collective-permute-done.6.refs_7_ = bf16[3,2,256,128]{3,2,1,0:T(8,128)(2,1)} collective-permute-done((bf16[3,2,256,128]{3,2,1,0:T(8,128)(2,1)}, bf16[3,2,256,128]{3,2,1,0:T(8,128)(2,1)}, u32[]{:S(2)}, u32[]{:S(2)}) %collective-permute-start.6) | collective-permute-done | bytes 393248 | tf_op jit(solution)/shard_map/ppermute | solution.py:42
  180.3 14.6 %attend_fwd.3 = (bf16[2,256,128]{2,1,0:T(8,128)(2,1)}, bf16[2,256,128]{2,1,0:T(8,128)(2,1)}, bf16[2,256,128]{2,1,0:T(8,128)(2,1)}, bf16[2,256,128]{2,1,0:T(8,128...) custom-call(s32[8]{0:T(128)} %_.21, ...), custom_call_target="tpu_custom_call" | custom-call | flops 137438953472 | bytes 67108864 | tf_op jit(solution)/shard_map/attend_fwd/pallas_call | solution.py:319
  201.8 9.8 %align_head.2.refs_10_ = bf16[8,2,256,128]{3,2,1,0:T(8,128)(2,1)} custom-call(s32[8]{0:T(128)} %_.21, s32[3]{0:T(128)} %pad_add_fusion.__.me_ref, bf16[8,2,256,128]{3,2,1,0:T(8,128)(2,1)} %all-to-all-done.1.refs_0_, bf16[4,2048,384]{2,1,0:T(8,128)(2,1)} %bitcast.4, bf16[2,256,1536]{2,1,0:T(8,128)(2,1)} %collective-permute-done.7.refs_4_.refs_2_.refs_9_, ...), custom_call_target="tpu_custom_call" | custom-call | flops 51539607552 | bytes 184549376 | tf_op jit(solution)/shard_map/align_head/pallas_call | solution.py:635
  211.6 17.1 %all-to-all-start.2 = ((bf16[8,2,256,128]{3,2,1,0:T(8,128)(2,1)}), bf16[8,2,256,128]{3,2,1,0:T(8,128)(2,1)S(1)}, u32[]{:S(2)}, u32[]{:S(2)}) async-start(bf16[8,2,256,128]{3,2,1,0:T(8,128)(2,1)} %align_head.2.refs_10_), calls=%async_computation.2 | async-start | bytes 2097152 | tf_op jit(solution)/shard_map/all_to_all | solution.py:39
  230.2 10.1 %align_head.3 = (bf16[2,256,128]{2,1,0:T(8,128)(2,1)}, bf16[2,256,128]{2,1,0:T(8,128)(2,1)}, bf16[2,256,128]{2,1,0:T(8,128)(2,1)}, bf16[2,256,128]{2,1,0:T(8,128...) custom-call(s32[8]{0:T(128)} %_.21, ...), custom_call_target="tpu_custom_call" | custom-call | flops 51539607552 | bytes 184549376 | tf_op jit(solution)/shard_map/align_head/pallas_call | solution.py:635
  246.3 3.4 collective-permute-done.16.refs_7_.refs_10_
  249.8 3.2 collective-permute-start.21
  254.0 26.7 %attend_bwd.2.refs_18_ = bf16[8,3,2,256,128]{4,3,2,1,0:T(8,128)(2,1)} custom-call(s32[8]{0:T(128)} %_.21, s32[3]{0:T(128)} %pad_add_fusion.__.me_ref, bf16[8,3,2,256,128]{4,3,2,1,0:T(8,128)(2,1)} %all-to-all-done.refs_0_, bf16[8,2,256,128]{3,2,1,0:T(8,128)(2,1)} %copy-done.9, f32[2,8,2048]{2,1,0:T(8,128)} %get-tuple-element.73.refs_1_.refs_2_, ...), custom_call_target="tpu_custom_call" | custom-call | flops 343597383680 | bytes 117440512 | tf_op jit(solution)/shard_map/attend_bwd/pallas_call | solution.py:502
  280.6 7.5 %all-to-all-start.3 = ((bf16[8,3,2,256,128]{4,3,2,1,0:T(8,128)(2,1)}), bf16[8,3,2,256,128]{4,3,2,1,0:T(8,128)(2,1)}, u32[]{:S(2)}, u32[]{:S(2)}) async-start(bf16[8,3,2,256,128]{4,3,2,1,0:T(8,128)(2,1)} %attend_bwd.2.refs_18_), calls=%async_computation.3 | async-start | bytes 6291456 | tf_op jit(solution)/shard_map/all_to_all | solution.py:39
  288.2 29.0 %attend_bwd.3 = (bf16[3,2,256,128]{3,2,1,0:T(8,128)(2,1)}, bf16[3,2,256,128]{3,2,1,0:T(8,128)(2,1)}, bf16[3,2,256,128]{3,2,1,0:T(8,128)(2,1)}, bf16[3,2,256,128]...) custom-call(s32[8]{0:T(128)} %_.21, ...), custom_call_target="tpu_custom_call" | custom-call | flops 343597383680 | bytes 117440512 | tf_op jit(solution)/shard_map/attend_bwd/pallas_call | solution.py:502
  322.3 26.2 %collective-permute-done.27.refs_3_.src = bf16[3,2,256,128]{3,2,1,0:T(8,128)(2,1)S(1)} collective-permute-done((bf16[3,2,256,128]{3,2,1,0:T(8,128)(2,1)}, bf16[3,2,256,128]{3,2,1,0:T(8,128)(2,1)S(1)}, u32[]{:S(2)}, u32[]{:S(2)}) %collective-permute-start.27) | collective-permute-done | bytes 393248 | tf_op jit(solution)/shard_map/ppermute | solution.py:42
  351.7 4.4 %all-to-all-done.3.refs_0_ = bf16[8,3,2,256,128]{4,3,2,1,0:T(8,128)(2,1)} async-done(((bf16[8,3,2,256,128]{4,3,2,1,0:T(8,128)(2,1)}), bf16[8,3,2,256,128]{4,3,2,1,0:T(8,128)(2,1)}, u32[]{:S(2)}, u32[]{:S(2)}) %all-to-all-start.3) | async-done | bytes 3145760 | tf_op jit(solution)/shard_map/all_to_all | solution.py:39
  356.1 5.2 %unpack.1 = (bf16[2,256,2048]{2,1,0:T(8,128)(2,1)}, bf16[2,256,2048]{2,1,0:T(8,128)(2,1)}, bf16[2,256,2048]{2,1,0:T(8,128)(2,1)}) custom-call(s32[8]{0:T(128)} %_.21, s32[3]{0:T(128)} %pad_add_fusion.__.me_ref, bf16[8,3,2,256,128]{4,3,2,1,0:T(8,128)(2,1)} %all-to-all-done.3.refs_0_, bf16[3,2,256,128]{3,2,1,0:T(8,128)(2,1)} %get-tuple-element.100.refs_1_.src, ...), custom_call_target="tpu_custom_call" | custom-call | bytes 100663296 | tf_op jit(solution)/shard_map/unpack/pallas_call | solution.py:178
  365.5 2.4 place.11
  367.8 30.3 %collective-permute-done.25.src = bf16[3,2,256,128]{3,2,1,0:T(8,128)(2,1)} collective-permute-done((bf16[3,2,256,128]{3,2,1,0:T(8,128)(2,1)}, bf16[3,2,256,128]{3,2,1,0:T(8,128)(2,1)}, u32[]{:S(2)}, u32[]{:S(2)}) %collective-permute-start.25) | collective-permute-done | bytes 393248 | tf_op jit(solution)/shard_map/ppermute | solution.py:42
  400.5 6.1 %collective-permute-done.24.src = bf16[3,2,256,128]{3,2,1,0:T(8,128)(2,1)} collective-permute-done((bf16[3,2,256,128]{3,2,1,0:T(8,128)(2,1)}, bf16[3,2,256,128]{3,2,1,0:T(8,128)(2,1)}, u32[]{:S(2)}, u32[]{:S(2)}) %collective-permute-start.24) | collective-permute-done | bytes 393248 | tf_op jit(solution)/shard_map/ppermute | solution.py:42
  409.0 7.7 %collective-permute-done.23.src = bf16[3,2,256,128]{3,2,1,0:T(8,128)(2,1)S(1)} collective-permute-done((bf16[3,2,256,128]{3,2,1,0:T(8,128)(2,1)}, bf16[3,2,256,128]{3,2,1,0:T(8,128)(2,1)S(1)}, u32[]{:S(2)}, u32[]{:S(2)}) %collective-permute-start.23) | collective-permute-done | bytes 393248 | tf_op jit(solution)/shard_map/ppermute | solution.py:42
  418.0 7.2 %collective-permute-done.22.src = bf16[3,2,256,128]{3,2,1,0:T(8,128)(2,1)S(1)} collective-permute-done((bf16[3,2,256,128]{3,2,1,0:T(8,128)(2,1)}, bf16[3,2,256,128]{3,2,1,0:T(8,128)(2,1)S(1)}, u32[]{:S(2)}, u32[]{:S(2)}) %collective-permute-start.22) | collective-permute-done | bytes 393248 | tf_op jit(solution)/shard_map/ppermute | solution.py:42
  (110 shorter events, 45.5 us)
Async XLA Ops:
  12.8 86.5 %all-to-all-start = ((bf16[8,3,2,256,128]{4,3,2,1,0:T(8,128)(2,1)}), bf16[8,3,2,256,128]{4,3,2,1,0:T(8,128)(2,1)}, u32[]{:S(2)}, u32[]{:S(2)}) async-start(bf16[8,3,2,256,128]{4,3,2,1,0:T(8,128)(2,1)} %pack.2.refs_24_._), calls=%async_computation | async-start | bytes 6291456 | tf_op jit(solution)/shard_map/all_to_all | solution.py:39
  18.6 41.3 %all-gather.4.cloned.1.call-start = ((), (), s32[]{:S(2)}) async-start(), calls=%async_computation.4 | async-start | bytes 1769472 | tf_op jit(solution)/shard_map/all_gather | solution.py:541
  19.3 182.5 %all-gather.6.cloned.1.call-start = ((), (), s32[]{:S(2)}) async-start(), calls=%async_computation.5 | async-start | bytes 7864320 | tf_op jit(solution)/shard_map/all_gather | solution.py:543
  23.8 70.0 %collective-permute-start.7 = (bf16[2,256,1536]{2,1,0:T(8,128)(2,1)}, bf16[2,256,1536]{2,1,0:T(8,128)(2,1)}, u32[]{:S(2)}, u32[]{:S(2)}) collective-permute-start(bf16[2,256,1536]{2,1,0:T(8,128)(2,1)} %layer_norm.1), channel_id=1, source_target_pairs={{0,16},{16,0},{1,17},{17,1},{2,18},{18,2},{3,19},{19,3},{4,20},{20... | collective-permute-start | bytes 4718600 | tf_op jit(solution)/shard_map/ppermute | solution.py:34
  28.7 31.3 %collective-permute-start = (bf16[3,2,256,128]{3,2,1,0:T(8,128)(2,1)}, bf16[3,2,256,128]{3,2,1,0:T(8,128)(2,1)S(1)}, u32[]{:S(2)}, u32[]{:S(2)}) collective-permute-start(bf16[3,2,256,128]{3,2,1,0:T(8,128)(2,1)} %get-tuple-element.65), channel_id=1, source_target_pairs={{0,2},{2,0},{4,6},{6,4},{8,10},{10,8},{12,14},{14,12},{1,3},{3,1},... | collective-permute-start | bytes 1179656 | tf_op jit(solution)/shard_map/ppermute | solution.py:42
  29.4 62.3 %collective-permute-start.1 = (bf16[3,2,256,128]{3,2,1,0:T(8,128)(2,1)}, bf16[3,2,256,128]{3,2,1,0:T(8,128)(2,1)S(1)}, u32[]{:S(2)}, u32[]{:S(2)}) collective-permute-start(bf16[3,2,256,128]{3,2,1,0:T(8,128)(2,1)} %get-tuple-element.66), channel_id=1, source_target_pairs={{0,4},{2,6},{4,0},{6,2},{8,12},{10,14},{12,8},{14,10},{1,5},{3,7},... | collective-permute-start | bytes 1179656 | tf_op jit(solution)/shard_map/ppermute | solution.py:42
  29.4 106.9 %collective-permute-start.2 = (bf16[3,2,256,128]{3,2,1,0:T(8,128)(2,1)}, bf16[3,2,256,128]{3,2,1,0:T(8,128)(2,1)}, u32[]{:S(2)}, u32[]{:S(2)}) collective-permute-start(bf16[3,2,256,128]{3,2,1,0:T(8,128)(2,1)} %get-tuple-element.67), channel_id=1, source_target_pairs={{0,6},{2,4},{4,2},{6,0},{8,14},{10,12},{12,10},{14,8},{1,7},{3,5},... | collective-permute-start | bytes 1179656 | tf_op jit(solution)/shard_map/ppermute | solution.py:42
  31.1 121.6 %collective-permute-start.3 = (bf16[3,2,256,128]{3,2,1,0:T(8,128)(2,1)}, bf16[3,2,256,128]{3,2,1,0:T(8,128)(2,1)}, u32[]{:S(2)}, u32[]{:S(2)}) collective-permute-start(bf16[3,2,256,128]{3,2,1,0:T(8,128)(2,1)} %get-tuple-element.68), channel_id=1, source_target_pairs={{0,8},{2,10},{4,12},{6,14},{8,0},{10,2},{12,4},{14,6},{1,9},{3,11}... | collective-permute-start | bytes 1179656 | tf_op jit(solution)/shard_map/ppermute | solution.py:42
  60.0 101.1 %collective-permute-start.4 = (bf16[3,2,256,128]{3,2,1,0:T(8,128)(2,1)}, bf16[3,2,256,128]{3,2,1,0:T(8,128)(2,1)}, u32[]{:S(2)}, u32[]{:S(2)}) collective-permute-start(bf16[3,2,256,128]{3,2,1,0:T(8,128)(2,1)} %get-tuple-element.69), channel_id=1, source_target_pairs={{0,10},{2,8},{4,14},{6,12},{8,2},{10,0},{12,6},{14,4},{1,11},{3,9}... | collective-permute-start | bytes 1179656 | tf_op jit(solution)/shard_map/ppermute | solution.py:42
  91.7 79.5 %collective-permute-start.5 = (bf16[3,2,256,128]{3,2,1,0:T(8,128)(2,1)}, bf16[3,2,256,128]{3,2,1,0:T(8,128)(2,1)}, u32[]{:S(2)}, u32[]{:S(2)}) collective-permute-start(bf16[3,2,256,128]{3,2,1,0:T(8,128)(2,1)} %get-tuple-element.70), channel_id=1, source_target_pairs={{0,12},{2,14},{4,8},{6,10},{8,4},{10,6},{12,0},{14,2},{1,13},{3,15... | collective-permute-start | bytes 1179656 | tf_op jit(solution)/shard_map/ppermute | solution.py:42
  93.7 86.5 %collective-permute-start.6 = (bf16[3,2,256,128]{3,2,1,0:T(8,128)(2,1)}, bf16[3,2,256,128]{3,2,1,0:T(8,128)(2,1)}, u32[]{:S(2)}, u32[]{:S(2)}) collective-permute-start(bf16[3,2,256,128]{3,2,1,0:T(8,128)(2,1)} %get-tuple-element.71), channel_id=1, source_target_pairs={{0,14},{2,12},{4,10},{6,8},{8,6},{10,4},{12,2},{14,0},{1,15},{3,13... | collective-permute-start | bytes 1179656 | tf_op jit(solution)/shard_map/ppermute | solution.py:42
  113.8 88.0 %all-to-all-start.1 = ((bf16[8,2,256,128]{3,2,1,0:T(8,128)(2,1)}), bf16[8,2,256,128]{3,2,1,0:T(8,128)(2,1)}, u32[]{:S(2)}, u32[]{:S(2)}) async-start(bf16[8,2,256,128]{3,2,1,0:T(8,128)(2,1)} %get-tuple-element.72.refs_8_), calls=%async_computation.1 | async-start | bytes 2097152 | tf_op jit(solution)/shard_map/all_to_all | solution.py:39
  195.1 33.7 %collective-permute-start.10 = (bf16[2,256,128]{2,1,0:T(8,128)(2,1)}, bf16[2,256,128]{2,1,0:T(8,128)(2,1)S(1)}, u32[]{:S(2)}, u32[]{:S(2)}) collective-permute-start(bf16[2,256,128]{2,1,0:T(8,128)(2,1)} %get-tuple-element.77), channel_id=1, source_target_pairs={{0,6},{2,4},{4,2},{6,0},{8,14},{10,12},{12,10},{14,8},{1,7},{3,5},... | collective-permute-start | bytes 393224 | tf_op jit(solution)/shard_map/ppermute | solution.py:42
  197.1 31.6 %collective-permute-start.11 = (bf16[2,256,128]{2,1,0:T(8,128)(2,1)}, bf16[2,256,128]{2,1,0:T(8,128)(2,1)S(1)}, u32[]{:S(2)}, u32[]{:S(2)}) collective-permute-start(bf16[2,256,128]{2,1,0:T(8,128)(2,1)} %get-tuple-element.78), channel_id=1, source_target_pairs={{0,8},{2,10},{4,12},{6,14},{8,0},{10,2},{12,4},{14,6},{1,9},{3,11}... | collective-permute-start | bytes 393224 | tf_op jit(solution)/shard_map/ppermute | solution.py:42
  197.1 31.7 %collective-permute-start.12 = (bf16[2,256,128]{2,1,0:T(8,128)(2,1)}, bf16[2,256,128]{2,1,0:T(8,128)(2,1)S(1)}, u32[]{:S(2)}, u32[]{:S(2)}) collective-permute-start(bf16[2,256,128]{2,1,0:T(8,128)(2,1)} %get-tuple-element.79), channel_id=1, source_target_pairs={{0,10},{2,8},{4,14},{6,12},{8,2},{10,0},{12,6},{14,4},{1,11},{3,9}... | collective-permute-start | bytes 393224 | tf_op jit(solution)/shard_map/ppermute | solution.py:42
  199.5 29.3 %collective-permute-start.13 = (bf16[2,256,128]{2,1,0:T(8,128)(2,1)}, bf16[2,256,128]{2,1,0:T(8,128)(2,1)S(1)}, u32[]{:S(2)}, u32[]{:S(2)}) collective-permute-start(bf16[2,256,128]{2,1,0:T(8,128)(2,1)} %get-tuple-element.80), channel_id=1, source_target_pairs={{0,12},{2,14},{4,8},{6,10},{8,4},{10,6},{12,0},{14,2},{1,13},{3,15... | collective-permute-start | bytes 393224 | tf_op jit(solution)/shard_map/ppermute | solution.py:42
  199.9 28.9 %collective-permute-start.14 = (bf16[2,256,128]{2,1,0:T(8,128)(2,1)}, bf16[2,256,128]{2,1,0:T(8,128)(2,1)S(1)}, u32[]{:S(2)}, u32[]{:S(2)}) collective-permute-start(bf16[2,256,128]{2,1,0:T(8,128)(2,1)} %get-tuple-element.81), channel_id=1, source_target_pairs={{0,14},{2,12},{4,10},{6,8},{8,6},{10,4},{12,2},{14,0},{1,15},{3,13... | collective-permute-start | bytes 393224 | tf_op jit(solution)/shard_map/ppermute | solution.py:42
  211.6 41.4 %all-to-all-start.2 = ((bf16[8,2,256,128]{3,2,1,0:T(8,128)(2,1)}), bf16[8,2,256,128]{3,2,1,0:T(8,128)(2,1)S(1)}, u32[]{:S(2)}, u32[]{:S(2)}) async-start(bf16[8,2,256,128]{3,2,1,0:T(8,128)(2,1)} %align_head.2.refs_10_), calls=%async_computation.2 | async-start | bytes 2097152 | tf_op jit(solution)/shard_map/all_to_all | solution.py:39
  240.7 9.0 %collective-permute-start.16 = (bf16[2,256,128]{2,1,0:T(8,128)(2,1)}, bf16[2,256,128]{2,1,0:T(8,128)(2,1)S(1)}, u32[]{:S(2)}, u32[]{:S(2)}) collective-permute-start(bf16[2,256,128]{2,1,0:T(8,128)(2,1)} %get-tuple-element.84), channel_id=1, source_target_pairs={{0,4},{2,6},{4,0},{6,2},{8,12},{10,14},{12,8},{14,10},{1,5},{3,7},... | collective-permute-start | bytes 393224 | tf_op jit(solution)/shard_map/ppermute | solution.py:42
  240.7 47.4 %collective-permute-start.17 = (bf16[2,256,128]{2,1,0:T(8,128)(2,1)}, bf16[2,256,128]{2,1,0:T(8,128)(2,1)}, u32[]{:S(2)}, u32[]{:S(2)}) collective-permute-start(bf16[2,256,128]{2,1,0:T(8,128)(2,1)} %get-tuple-element.85), channel_id=1, source_target_pairs={{0,6},{2,4},{4,2},{6,0},{8,14},{10,12},{12,10},{14,8},{1,7},{3,5},... | collective-permute-start | bytes 393224 | tf_op jit(solution)/shard_map/ppermute | solution.py:42
  242.5 45.6 %collective-permute-start.18 = (bf16[2,256,128]{2,1,0:T(8,128)(2,1)}, bf16[2,256,128]{2,1,0:T(8,128)(2,1)}, u32[]{:S(2)}, u32[]{:S(2)}) collective-permute-start(bf16[2,256,128]{2,1,0:T(8,128)(2,1)} %get-tuple-element.86), channel_id=1, source_target_pairs={{0,8},{2,10},{4,12},{6,14},{8,0},{10,2},{12,4},{14,6},{1,9},{3,11}... | collective-permute-start | bytes 393224 | tf_op jit(solution)/shard_map/ppermute | solution.py:42
  244.6 43.5 %collective-permute-start.19 = (bf16[2,256,128]{2,1,0:T(8,128)(2,1)}, bf16[2,256,128]{2,1,0:T(8,128)(2,1)}, u32[]{:S(2)}, u32[]{:S(2)}) collective-permute-start(bf16[2,256,128]{2,1,0:T(8,128)(2,1)} %get-tuple-element.87), channel_id=1, source_target_pairs={{0,10},{2,8},{4,14},{6,12},{8,2},{10,0},{12,6},{14,4},{1,11},{3,9}... | collective-permute-start | bytes 393224 | tf_op jit(solution)/shard_map/ppermute | solution.py:42
  245.1 43.0 %collective-permute-start.20 = (bf16[2,256,128]{2,1,0:T(8,128)(2,1)}, bf16[2,256,128]{2,1,0:T(8,128)(2,1)}, u32[]{:S(2)}, u32[]{:S(2)}) collective-permute-start(bf16[2,256,128]{2,1,0:T(8,128)(2,1)} %get-tuple-element.88), channel_id=1, source_target_pairs={{0,12},{2,14},{4,8},{6,10},{8,4},{10,6},{12,0},{14,2},{1,13},{3,15... | collective-permute-start | bytes 393224 | tf_op jit(solution)/shard_map/ppermute | solution.py:42
  249.8 38.4 %collective-permute-start.21 = (bf16[2,256,128]{2,1,0:T(8,128)(2,1)}, bf16[2,256,128]{2,1,0:T(8,128)(2,1)}, u32[]{:S(2)}, u32[]{:S(2)}) collective-permute-start(bf16[2,256,128]{2,1,0:T(8,128)(2,1)} %get-tuple-element.89), channel_id=1, source_target_pairs={{0,14},{2,12},{4,10},{6,8},{8,6},{10,4},{12,2},{14,0},{1,15},{3,13... | collective-permute-start | bytes 393224 | tf_op jit(solution)/shard_map/ppermute | solution.py:42
  280.6 75.5 %all-to-all-start.3 = ((bf16[8,3,2,256,128]{4,3,2,1,0:T(8,128)(2,1)}), bf16[8,3,2,256,128]{4,3,2,1,0:T(8,128)(2,1)}, u32[]{:S(2)}, u32[]{:S(2)}) async-start(bf16[8,3,2,256,128]{4,3,2,1,0:T(8,128)(2,1)} %attend_bwd.2.refs_18_), calls=%async_computation.3 | async-start | bytes 6291456 | tf_op jit(solution)/shard_map/all_to_all | solution.py:39
  317.2 31.3 %collective-permute-start.27 = (bf16[3,2,256,128]{3,2,1,0:T(8,128)(2,1)}, bf16[3,2,256,128]{3,2,1,0:T(8,128)(2,1)S(1)}, u32[]{:S(2)}, u32[]{:S(2)}) collective-permute-start(bf16[3,2,256,128]{3,2,1,0:T(8,128)(2,1)} %get-tuple-element.98), channel_id=1, source_target_pairs={{0,4},{2,6},{4,0},{6,2},{8,12},{10,14},{12,8},{14,10},{1,5},{3,7},... | collective-permute-start | bytes 1179656 | tf_op jit(solution)/shard_map/ppermute | solution.py:42
  317.3 33.1 %collective-permute-start.28 = (bf16[3,2,256,128]{3,2,1,0:T(8,128)(2,1)}, bf16[3,2,256,128]{3,2,1,0:T(8,128)(2,1)S(1)}, u32[]{:S(2)}, u32[]{:S(2)}) collective-permute-start(bf16[3,2,256,128]{3,2,1,0:T(8,128)(2,1)} %get-tuple-element.99), channel_id=1, source_target_pairs={{0,2},{2,0},{4,6},{6,4},{8,10},{10,8},{12,14},{14,12},{1,3},{3,1},... | collective-permute-start | bytes 1179656 | tf_op jit(solution)/shard_map/ppermute | solution.py:42
  317.7 47.8 %collective-permute-start.26 = (bf16[3,2,256,128]{3,2,1,0:T(8,128)(2,1)}, bf16[3,2,256,128]{3,2,1,0:T(8,128)(2,1)}, u32[]{:S(2)}, u32[]{:S(2)}) collective-permute-start(bf16[3,2,256,128]{3,2,1,0:T(8,128)(2,1)} %get-tuple-element.97), channel_id=1, source_target_pairs={{0,6},{2,4},{4,2},{6,0},{8,14},{10,12},{12,10},{14,8},{1,7},{3,5},... | collective-permute-start | bytes 1179656 | tf_op jit(solution)/shard_map/ppermute | solution.py:42
  319.2 78.9 %collective-permute-start.25 = (bf16[3,2,256,128]{3,2,1,0:T(8,128)(2,1)}, bf16[3,2,256,128]{3,2,1,0:T(8,128)(2,1)}, u32[]{:S(2)}, u32[]{:S(2)}) collective-permute-start(bf16[3,2,256,128]{3,2,1,0:T(8,128)(2,1)} %get-tuple-element.96), channel_id=1, source_target_pairs={{0,8},{2,10},{4,12},{6,14},{8,0},{10,2},{12,4},{14,6},{1,9},{3,11}... | collective-permute-start | bytes 1179656 | tf_op jit(solution)/shard_map/ppermute | solution.py:42
  321.4 85.3 %collective-permute-start.24 = (bf16[3,2,256,128]{3,2,1,0:T(8,128)(2,1)}, bf16[3,2,256,128]{3,2,1,0:T(8,128)(2,1)}, u32[]{:S(2)}, u32[]{:S(2)}) collective-permute-start(bf16[3,2,256,128]{3,2,1,0:T(8,128)(2,1)} %get-tuple-element.95), channel_id=1, source_target_pairs={{0,10},{2,8},{4,14},{6,12},{8,2},{10,0},{12,6},{14,4},{1,11},{3,9}... | collective-permute-start | bytes 1179656 | tf_op jit(solution)/shard_map/ppermute | solution.py:42
  348.5 68.1 %collective-permute-start.23 = (bf16[3,2,256,128]{3,2,1,0:T(8,128)(2,1)}, bf16[3,2,256,128]{3,2,1,0:T(8,128)(2,1)S(1)}, u32[]{:S(2)}, u32[]{:S(2)}) collective-permute-start(bf16[3,2,256,128]{3,2,1,0:T(8,128)(2,1)} %get-tuple-element.94), channel_id=1, source_target_pairs={{0,12},{2,14},{4,8},{6,10},{8,4},{10,6},{12,0},{14,2},{1,13},{3,15... | collective-permute-start | bytes 1179656 | tf_op jit(solution)/shard_map/ppermute | solution.py:42
  350.5 74.8 %collective-permute-start.22 = (bf16[3,2,256,128]{3,2,1,0:T(8,128)(2,1)}, bf16[3,2,256,128]{3,2,1,0:T(8,128)(2,1)S(1)}, u32[]{:S(2)}, u32[]{:S(2)}) collective-permute-start(bf16[3,2,256,128]{3,2,1,0:T(8,128)(2,1)} %get-tuple-element.93), channel_id=1, source_target_pairs={{0,14},{2,12},{4,10},{6,8},{8,6},{10,4},{12,2},{14,0},{1,15},{3,13... | collective-permute-start | bytes 1179656 | tf_op jit(solution)/shard_map/ppermute | solution.py:42
  (26 other events, 139.3 us)
Sparse Core Ops, SparseCore 0:
  21.1 38.8 all-gather.3
  61.8 76.1 all-gather.5
